TPU v7x, 128 devices: a whole 4x4x4 slice. The times are simulated.
128 devices in a mesh: seq: 32 (over z, y, core), grp: 4 (over x).
Axes of the slice: x: 4, y: 4, z: 4, core: 2. Of those that a mesh axis runs over, the one named last changes fastest.
Arguments:
- query_states: bfloat16 [64, 16384, 128], P('grp', 'seq'), may hold values from -6 to 6
- key_states: bfloat16 [8, 16384, 128], P('grp', 'seq'), may hold values from -6 to 6
- value_states: bfloat16 [8, 16384, 128], P('grp', 'seq'), may hold values from -6 to 6
- tile_keys: int32 [64, 128, 16], P('grp'), may hold values from 0 to 127, as said below
- tile_count: int32 [64, 128], P('grp'), may hold values from 1 to 16, as said below
- out_weight: bfloat16 [8192, 4096], P('grp'), may hold values from -0.0625 to 0.0625
Outputs:
- projected: bfloat16 [16384, 4096], P(('seq', 'grp'))
Inputs may be any that keep to these rules, and one draw needn't show every extreme that they name: `tile_count`: for each head and query block, at least one and at most 16 key blocks are named; 16 is reached. `tile_keys`: for head h and query block i, slots 0 to tile_count[h, i] - 1 name distinct key blocks in falling order, the first being block i itself and none after i; the remaining slots hold 0.
All inputs are finite; a program needn't handle non-finite values.
Results may differ from a plain program's by a relative error of at most 0.0056.
Values may be sent and summed in bfloat16 or wider, within the bound.
No kernel may reach another device: no remote copies, remote signals or barrier semaphores. Data moves between devices by JAX's collectives and lax.ppermute only.
A program may use at most 128 MiB of HBM per device.

v0:
```python
import jax
import jax.numpy as jnp
from jax import lax
from jax.sharding import PartitionSpec as P

HEADS = 64
KVH = 8
BLK = 128


def allowed_mask(used_slots, count_batch, block_batch, block_rows):
    slot_span = used_slots.shape[1]
    column = jnp.arange(slot_span * block_rows, dtype=jnp.int32)
    slot_of = column // block_rows
    inner_pos = column % block_rows
    key_block = used_slots[:, slot_of]
    live_slot = slot_of[None, :] < count_batch[:, None]
    own_block = key_block == block_batch[:, None]
    row_index = jnp.arange(block_rows, dtype=jnp.int32)
    earlier = inner_pos[None, :] <= row_index[:, None]
    return live_slot[:, None, :] & (jnp.logical_not(own_block)[:, None, :] | earlier[None, :, :])


def attend_tiles(
    slot_span,
    block_total,
    key_table,
    value_table,
    query_batch,
    list_batch,
    count_batch,
    block_batch,
    select_batch,
):
    batch_size, block_rows, head_width = query_batch.shape
    table_rows = (select_batch[:, None] * block_total + list_batch).reshape(-1)
    key_tiles = jnp.take(key_table, table_rows, axis=0).reshape(
        batch_size, slot_span * block_rows, head_width
    )
    value_tiles = jnp.take(value_table, table_rows, axis=0).reshape(
        batch_size, slot_span * block_rows, head_width
    )
    scores = jnp.einsum(
        "gqd,gkd->gqk", query_batch, key_tiles, preferred_element_type=jnp.float32
    ) * head_width ** (-0.5)
    allowed = allowed_mask(list_batch, count_batch, block_batch, block_rows)
    scores = jnp.where(allowed, scores, -jnp.inf)
    row_top = jnp.max(scores, axis=-1, keepdims=True)
    weights = jnp.exp(scores - row_top)
    row_total = jnp.sum(weights, axis=-1, keepdims=True)
    rounded = weights.astype(jnp.bfloat16)
    summed = jnp.einsum("gqk,gkd->gqd", rounded, value_tiles, preferred_element_type=jnp.float32)
    return (summed / row_total).astype(jnp.bfloat16)


def run_blocks(
    query_flat,
    tile_lists,
    tile_counts,
    global_block,
    kv_select,
    key_table,
    value_table,
    block_total,
):
    total_blocks, block_rows, head_width = query_flat.shape
    slot_total = tile_lists.shape[1]
    step_total = total_blocks // 8

    def batched(array):
        return array.reshape((step_total, 8) + array.shape[1:])

    def one_step(packed):
        query_batch, list_batch, count_batch, block_batch, select_batch = packed
        return attend_tiles(
            slot_total,
            block_total,
            key_table,
            value_table,
            query_batch,
            list_batch,
            count_batch,
            block_batch,
            select_batch,
        )

    result = lax.map(
        one_step,
        (
            batched(query_flat),
            batched(tile_lists),
            batched(tile_counts),
            batched(global_block),
            batched(kv_select),
        ),
    )
    return result.reshape(total_blocks, block_rows, head_width)


def body(query_states, key_states, value_states, tile_keys, tile_count, out_weight):
    head_group, row_count, head_width = query_states.shape
    seq_size = lax.axis_size("seq")
    seq_place = lax.axis_index("seq")
    head_ratio = HEADS // KVH
    seq_total = row_count * seq_size
    block_total = seq_total // BLK
    slot_total = tile_keys.shape[2]
    kv_pair = jnp.stack([key_states, value_states])
    unit_count = 2 * head_group // seq_size
    half_rows = row_count // 2
    outgoing = query_states.reshape(head_group * 2, half_rows, head_width)
    owned_rows = lax.all_to_all(outgoing, "seq", split_axis=0, concat_axis=1, tiled=True)
    unit_ids = seq_place * unit_count + jnp.arange(unit_count, dtype=jnp.int32)
    head_ids = unit_ids // 2
    parity = unit_ids % 2
    per_source = half_rows // BLK
    local_blocks = row_count // BLK
    block_index = jnp.arange(seq_total // 2 // BLK, dtype=jnp.int32)
    global_block = (
        (block_index // per_source)[None, :] * local_blocks
        + parity[:, None] * per_source
        + (block_index % per_source)[None, :]
    )
    tile_lists = tile_keys[head_ids[:, None], global_block]
    tile_counts = tile_count[head_ids[:, None], global_block]
    kv_head = seq_place * unit_count // 2 // head_ratio
    all_kv = lax.all_gather(kv_pair, "seq", axis=2, tiled=True)
    own_kv = lax.dynamic_index_in_dim(all_kv, kv_head, 1, keepdims=False)
    key_table = own_kv[0].reshape(block_total, BLK * head_width)
    value_table = own_kv[1].reshape(block_total, BLK * head_width)
    block_count = unit_count * (seq_total // 2 // BLK)
    attended = run_blocks(
        owned_rows.reshape(block_count, BLK, head_width),
        tile_lists.reshape(block_count, slot_total),
        tile_counts.reshape(block_count),
        global_block.reshape(block_count),
        jnp.zeros((block_count,), jnp.int32),
        key_table,
        value_table,
        block_total,
    )
    returned = lax.all_to_all(
        attended.reshape(unit_count, seq_total // 2, head_width),
        "seq",
        split_axis=1,
        concat_axis=0,
        tiled=True,
    )
    local_out = returned.reshape(head_group, row_count, head_width)
    proj_weight = out_weight.reshape(head_group, head_width, out_weight.shape[1])
    summed = lax.psum_scatter(
        jnp.einsum("hrd,hde->re", local_out, proj_weight, preferred_element_type=jnp.float32),
        "grp",
        scatter_dimension=0,
        tiled=True,
    )
    return summed.astype(jnp.bfloat16)


def solution(mesh):
    placed = (
        P("grp", "seq", None),
        P("grp", "seq", None),
        P("grp", "seq", None),
        P("grp", None, None),
        P("grp", None),
        P("grp", None),
    )
    return jax.shard_map(
        body, mesh=mesh, in_specs=placed, out_specs=P(("seq", "grp"), None), check_vma=False
    )
```

profile of v0, /device:TPU:1, one launch (start us, length us, event | category | flops | bytes accessed | tf_op | source)
XLA Modules:
  0.0 822.6 jit_solution(4519884534655295813)
XLA Ops:
  8.5 9.7 %all-to-all-start = ((bf16[32,256,128]{2,1,0:T(8,128)(2,1)}), bf16[32,256,128]{2,1,0:T(8,128)(2,1)}, u32[]{:S(2)}, u32[]{:S(2)}) async-start(bf16[32,256,128]{2,1,0:T(8,128)(2,1)} %bitcast.68), calls=%async_computation | async-start | bytes 4194304 | tf_op jit(solution)/shard_map/all_to_all | solution.py:112
  20.5 80.0 %all-gather.2.cloned.1.call-done = bf16[2,2,16384,128]{3,2,1,0:T(8,128)(2,1)} async-done(((bf16[2,2,512,128]{3,2,1,0:T(8,128)(2,1)}), bf16[2,2,16384,128]{3,2,1,0:T(8,128)(2,1)}) %all-gather.2.cloned.1.call-update) | async-done | bytes 16777232 | tf_op jit(solution)/shard_map/all_gather | solution.py:127
  120.8 502.2 %while.12 = (s32[]{:T(128)}, bf16[8,8,128,128]{3,2,1,0:T(8,128)(2,1)}, s32[8,8]{1,0:T(8,128)S(1)}, s32[8,8,16]{2,1,0:T(8,128)S(1)}, s32[8,8]{1,0:T(8,128)S(1)}, ...) while((s32[]{:T(128)}, ...), condition=%wide.region_3.5_spmd, body=%wide.region_0.4_spmd.sunk | while | flops 1114214528 | bytes 102694480 | solution.py:87
  120.9 11.5 %gather_fusion = bf16[128,16384]{1,0:T(8,128)(2,1)} fusion(bf16[128,16384]{1,0:T(8,128)(2,1)} %get-tuple-element.220, s32[1024]{0:T(1024)S(1)} %pad_clamp_fusion.2), kind=kCustom, calls=%fused_computation.clone.clone.1 | custom fusion | bytes 8389120 | tf_op jit(solution)/shard_map/while/body/eval_jaxpr/jit(_take)/gather | solution.py:37
  132.4 11.5 %gather_fusion.1 = bf16[128,16384]{1,0:T(8,128)(2,1)} fusion(bf16[128,16384]{1,0:T(8,128)(2,1)} %get-tuple-element.221, s32[1024]{0:T(1024)S(1)} %pad_clamp_fusion.2), kind=kCustom, calls=%fused_computation.1.clone.clone.1 | custom fusion | bytes 8389120 | tf_op jit(solution)/shard_map/while/body/eval_jaxpr/jit(_take)/gather | solution.py:40
  143.9 7.5 broadcast_select_fusion.3
  183.7 11.5 %gather_fusion = bf16[128,16384]{1,0:T(8,128)(2,1)} fusion(bf16[128,16384]{1,0:T(8,128)(2,1)} %get-tuple-element.220, s32[1024]{0:T(1024)S(1)} %pad_clamp_fusion.2), kind=kCustom, calls=%fused_computation.clone.clone.1 | custom fusion | bytes 8389120 | tf_op jit(solution)/shard_map/while/body/eval_jaxpr/jit(_take)/gather | solution.py:37
  195.2 11.5 %gather_fusion.1 = bf16[128,16384]{1,0:T(8,128)(2,1)} fusion(bf16[128,16384]{1,0:T(8,128)(2,1)} %get-tuple-element.221, s32[1024]{0:T(1024)S(1)} %pad_clamp_fusion.2), kind=kCustom, calls=%fused_computation.1.clone.clone.1 | custom fusion | bytes 8389120 | tf_op jit(solution)/shard_map/while/body/eval_jaxpr/jit(_take)/gather | solution.py:40
  206.7 7.5 broadcast_select_fusion.3
  246.5 11.5 %gather_fusion = bf16[128,16384]{1,0:T(8,128)(2,1)} fusion(bf16[128,16384]{1,0:T(8,128)(2,1)} %get-tuple-element.220, s32[1024]{0:T(1024)S(1)} %pad_clamp_fusion.2), kind=kCustom, calls=%fused_computation.clone.clone.1 | custom fusion | bytes 8389120 | tf_op jit(solution)/shard_map/while/body/eval_jaxpr/jit(_take)/gather | solution.py:37
  258.0 11.5 %gather_fusion.1 = bf16[128,16384]{1,0:T(8,128)(2,1)} fusion(bf16[128,16384]{1,0:T(8,128)(2,1)} %get-tuple-element.221, s32[1024]{0:T(1024)S(1)} %pad_clamp_fusion.2), kind=kCustom, calls=%fused_computation.1.clone.clone.1 | custom fusion | bytes 8389120 | tf_op jit(solution)/shard_map/while/body/eval_jaxpr/jit(_take)/gather | solution.py:40
  269.5 7.5 broadcast_select_fusion.3
  309.3 11.5 %gather_fusion = bf16[128,16384]{1,0:T(8,128)(2,1)} fusion(bf16[128,16384]{1,0:T(8,128)(2,1)} %get-tuple-element.220, s32[1024]{0:T(1024)S(1)} %pad_clamp_fusion.2), kind=kCustom, calls=%fused_computation.clone.clone.1 | custom fusion | bytes 8389120 | tf_op jit(solution)/shard_map/while/body/eval_jaxpr/jit(_take)/gather | solution.py:37
  320.8 11.5 %gather_fusion.1 = bf16[128,16384]{1,0:T(8,128)(2,1)} fusion(bf16[128,16384]{1,0:T(8,128)(2,1)} %get-tuple-element.221, s32[1024]{0:T(1024)S(1)} %pad_clamp_fusion.2), kind=kCustom, calls=%fused_computation.1.clone.clone.1 | custom fusion | bytes 8389120 | tf_op jit(solution)/shard_map/while/body/eval_jaxpr/jit(_take)/gather | solution.py:40
  332.3 7.5 broadcast_select_fusion.3
  372.0 11.5 %gather_fusion = bf16[128,16384]{1,0:T(8,128)(2,1)} fusion(bf16[128,16384]{1,0:T(8,128)(2,1)} %get-tuple-element.220, s32[1024]{0:T(1024)S(1)} %pad_clamp_fusion.2), kind=kCustom, calls=%fused_computation.clone.clone.1 | custom fusion | bytes 8389120 | tf_op jit(solution)/shard_map/while/body/eval_jaxpr/jit(_take)/gather | solution.py:37
  383.5 11.5 %gather_fusion.1 = bf16[128,16384]{1,0:T(8,128)(2,1)} fusion(bf16[128,16384]{1,0:T(8,128)(2,1)} %get-tuple-element.221, s32[1024]{0:T(1024)S(1)} %pad_clamp_fusion.2), kind=kCustom, calls=%fused_computation.1.clone.clone.1 | custom fusion | bytes 8389120 | tf_op jit(solution)/shard_map/while/body/eval_jaxpr/jit(_take)/gather | solution.py:40
  395.0 7.5 broadcast_select_fusion.3
  434.8 11.5 %gather_fusion = bf16[128,16384]{1,0:T(8,128)(2,1)} fusion(bf16[128,16384]{1,0:T(8,128)(2,1)} %get-tuple-element.220, s32[1024]{0:T(1024)S(1)} %pad_clamp_fusion.2), kind=kCustom, calls=%fused_computation.clone.clone.1 | custom fusion | bytes 8389120 | tf_op jit(solution)/shard_map/while/body/eval_jaxpr/jit(_take)/gather | solution.py:37
  446.3 11.5 %gather_fusion.1 = bf16[128,16384]{1,0:T(8,128)(2,1)} fusion(bf16[128,16384]{1,0:T(8,128)(2,1)} %get-tuple-element.221, s32[1024]{0:T(1024)S(1)} %pad_clamp_fusion.2), kind=kCustom, calls=%fused_computation.1.clone.clone.1 | custom fusion | bytes 8389120 | tf_op jit(solution)/shard_map/while/body/eval_jaxpr/jit(_take)/gather | solution.py:40
  457.8 7.5 broadcast_select_fusion.3
  497.6 11.5 %gather_fusion = bf16[128,16384]{1,0:T(8,128)(2,1)} fusion(bf16[128,16384]{1,0:T(8,128)(2,1)} %get-tuple-element.220, s32[1024]{0:T(1024)S(1)} %pad_clamp_fusion.2), kind=kCustom, calls=%fused_computation.clone.clone.1 | custom fusion | bytes 8389120 | tf_op jit(solution)/shard_map/while/body/eval_jaxpr/jit(_take)/gather | solution.py:37
  509.1 11.5 %gather_fusion.1 = bf16[128,16384]{1,0:T(8,128)(2,1)} fusion(bf16[128,16384]{1,0:T(8,128)(2,1)} %get-tuple-element.221, s32[1024]{0:T(1024)S(1)} %pad_clamp_fusion.2), kind=kCustom, calls=%fused_computation.1.clone.clone.1 | custom fusion | bytes 8389120 | tf_op jit(solution)/shard_map/while/body/eval_jaxpr/jit(_take)/gather | solution.py:40
  520.6 7.5 broadcast_select_fusion.3
  560.4 11.5 %gather_fusion = bf16[128,16384]{1,0:T(8,128)(2,1)} fusion(bf16[128,16384]{1,0:T(8,128)(2,1)} %get-tuple-element.220, s32[1024]{0:T(1024)S(1)} %pad_clamp_fusion.2), kind=kCustom, calls=%fused_computation.clone.clone.1 | custom fusion | bytes 8389120 | tf_op jit(solution)/shard_map/while/body/eval_jaxpr/jit(_take)/gather | solution.py:37
  571.9 11.5 %gather_fusion.1 = bf16[128,16384]{1,0:T(8,128)(2,1)} fusion(bf16[128,16384]{1,0:T(8,128)(2,1)} %get-tuple-element.221, s32[1024]{0:T(1024)S(1)} %pad_clamp_fusion.2), kind=kCustom, calls=%fused_computation.1.clone.clone.1 | custom fusion | bytes 8389120 | tf_op jit(solution)/shard_map/while/body/eval_jaxpr/jit(_take)/gather | solution.py:40
  583.4 7.5 broadcast_select_fusion.3
  623.0 7.5 copy.22
  631.0 45.2 %reduce = bf16[8192,128]{1,0:T(8,128)(2,1)S(1)} reduce(bf16[8192,1,128]{2,1,0:T(2,128)(2,1)} %bitcast.64, bf16[]{:T(256)} %broadcast.451), dimensions={1}, to_apply=%bitcast.47.reduce_sub_computation | reduce | bytes 4194306
  678.2 33.8 %all_to_all.8 = bf16[32,2,16384]{2,1,0:T(2,128)(2,1)S(1)} all-to-all(bf16[32,2,16384]{2,1,0:T(2,128)(2,1)} %reshape.327), channel_id=1, replica_groups=mesh['seq'=32,'grp'=4] {'seq'}, dimensions={0} | all-to-all | bytes 4194304 | tf_op jit(solution)/shard_map/all_to_all | solution.py:142
  721.2 13.8 %convolution_bitcast_fusion = f32[512,4096]{1,0:T(8,128)} fusion(bf16[16,512,128]{2,1,0:T(8,128)(2,1)S(1)} %bitcast.67, bf16[16,128,4096]{2,1,0:T(8,128)(2,1)} %bitcast.73), kind=kOutput, calls=%fused_computation.54 | convolution fusion | flops 8589934592 | bytes 27262976 | tf_op jit(solution)/shard_map/hrd,hde->re/dot_general | solution.py:152
  735.1 78.0 %reduce-scatter.2.cloned.1.call-done = f32[128,4096]{1,0:T(8,128)} async-done(((f32[512,4096]{1,0:T(8,128)}), f32[128,4096]{1,0:T(8,128)}) %reduce-scatter.2.cloned.1.call-update) | async-done | bytes 2097168 | tf_op jit(solution)/shard_map/reduce_scatter | solution.py:151
  (221 shorter events, 296.7 us)
Async XLA Ops:
  6.5 11.8 %copy-start = (s32[16,128]{1,0:T(8,128)S(1)}, s32[16,128]{1,0:T(8,128)}, u32[]{:S(2)}) copy-start(s32[16,128]{1,0:T(8,128)} %param.14) | copy-start | bytes 24580
  6.5 12.7 %copy-start.3 = (s32[16,128,16]{1,2,0:T(8,128)S(1)}, s32[16,128,16]{1,2,0:T(8,128)}, u32[]{:S(2)}) copy-start(s32[16,128,16]{1,2,0:T(8,128)} %param.13) | copy-start | bytes 393220
  6.5 93.9 %all-gather.2.cloned.1.call-start = ((), (), s32[]{:S(2)}) async-start(), calls=%async_computation.3 | async-start | bytes 17301504 | tf_op jit(solution)/shard_map/all_gather | solution.py:127
  8.5 112.3 %all-to-all-start = ((bf16[32,256,128]{2,1,0:T(8,128)(2,1)}), bf16[32,256,128]{2,1,0:T(8,128)(2,1)}, u32[]{:S(2)}, u32[]{:S(2)}) async-start(bf16[32,256,128]{2,1,0:T(8,128)(2,1)} %bitcast.68), calls=%async_computation | async-start | bytes 4194304 | tf_op jit(solution)/shard_map/all_to_all | solution.py:112
  18.2 794.9 %reduce-scatter.2.cloned.1.call-start = ((), (), s32[]{:S(2)}) async-start(), calls=%async_computation.4 | async-start | bytes 10485760 | tf_op jit(solution)/shard_map/reduce_scatter | solution.py:151
  176.8 3.0 copy-start.2
  239.5 3.0 copy-start.2
  302.3 3.0 copy-start.2
  365.1 3.0 copy-start.2
  427.9 3.0 copy-start.2
  490.6 3.0 copy-start.2
  553.4 3.0 copy-start.2
  616.2 3.0 copy-start.2
  735.0 80.7 %copy-start.1 = (s32[16,128]{1,0:T(8,128)S(1)}, s32[16,128]{1,0:T(8,128)}, u32[]{:S(2)}) copy-start(s32[16,128]{1,0:T(8,128)} %param.14) | copy-start | bytes 24580
Sparse Core Ops, SparseCore 0:
  9.7 90.7 all-gather.1
  735.2 77.8 reduce-scatter.1
where the time goes:
time: 827 us; the launch traced here: 823 us
  local copies, waits for them, and re-layouts  392 us (47%)
  waiting for transfers between devices  158 us (19%)
  other arithmetic  137 us (17%)
  matrix products  78 us (9%)
  blocking collectives  33.8 us (4%)
  between operations  13.5 us (2%)
  starting transfers between devices  9.71 us (1%)
    gather x8, local copies, waits for them, and re-layouts, attend_tiles(): jnp.take(value_table, table_rows, axis=0)  92 us
    gather x8, local copies, waits for them, and re-layouts, attend_tiles(): jnp.take(key_table, table_rows, axis=0)  91.9 us
    all_gather x1, waiting for transfers between devices, body(): all_kv = lax.all_gather(kv_pair, 'seq', axis=2, tiled=True)  80 us
    reduce_scatter x1, waiting for transfers between devices, body(): lax.psum_scatter(jnp.einsum('hrd,hde->re', local_out, proj_weight, prefer...  78 us
    select_n x16, other arithmetic, attend_tiles(): jnp.take(key_table, table_rows, axis=0)  59.8 us
    reshape x8, local copies, waits for them, and re-layouts, attend_tiles(): jnp.take(value_table, table_rows, axis=0)  59.2 us
    reshape x8, local copies, waits for them, and re-layouts, attend_tiles(): jnp.take(key_table, table_rows, axis=0)  59 us
    unnamed x1, other arithmetic  45.2 us
  transfers between devices with their start and end apart: 3, of which 2 were waited for; matrix products, arithmetic and copies ran while one was open for 3% of the time, Pallas kernels for 0%

commit v1 on v0

v1 whole, which is shorter than its diff:
```python
import math

import jax
import jax.numpy as jnp
from jax import lax
from jax.experimental import pallas as pl
from jax.experimental.pallas import tpu as pltpu
from jax.sharding import PartitionSpec as P

BLK = 128
SLOTS = 16
EXP2_SCALE = float(BLK ** -0.5 * math.log2(math.e))
LOW = -1e30


def attention_kernel(head_count, block_count, kv_ratio, lists, counts, q_ref, table_ref, out_ref, score_a, score_b, top_a, top_b):
    couples_per_block = head_count // 2
    couple_total = couples_per_block * block_count
    lanes = 2 * BLK
    key_row = lax.broadcasted_iota(jnp.int32, (BLK, lanes), 0)
    query_row = lax.broadcasted_iota(jnp.int32, (BLK, lanes), 1) % BLK
    lane = lax.broadcasted_iota(jnp.int32, (1, lanes), 1)
    zero = jnp.zeros((BLK, BLK), jnp.bfloat16)

    def place(couple):
        return couple // couples_per_block, 2 * (couple % couples_per_block)

    def pair_ids(couple):
        block, head = place(couple)
        return head * block_count + block, (head + 1) * block_count + block

    def live(couple):
        a, b = pair_ids(couple)
        return jnp.where(lane < BLK, counts[a], counts[b])

    def score_all(couple, score_ref, top_ref):
        block, head = place(couple)
        a, b = pair_ids(couple)
        rows = pl.ds(pl.multiple_of(block * BLK, BLK), BLK)
        qa = q_ref[head, rows, :].T
        qb = q_ref[head + 1, rows, :].T
        queries = jnp.concatenate(
            [jnp.concatenate([qa, zero], 1), jnp.concatenate([zero, qb], 1)], 0
        )
        keys = jnp.concatenate(
            [
                jnp.concatenate(
                    [table_ref[lists[a * SLOTS + n]], table_ref[lists[b * SLOTS + n]]], 1
                )
                for n in range(SLOTS)
            ],
            0,
        )
        scores = jnp.dot(keys, queries, preferred_element_type=jnp.float32)
        count = live(couple)
        top = None
        for n in range(SLOTS):
            tile = scores[n * BLK : (n + 1) * BLK]
            if n == 0:
                tile = jnp.where(key_row <= query_row, tile, LOW)
                top = tile.reshape(16, 8, lanes).max(0)
            else:
                best = tile.reshape(16, 8, lanes).max(0)
                top = jnp.maximum(top, jnp.where(n < count, best, LOW))
            score_ref[n * BLK : (n + 1) * BLK, :] = tile
        top_ref[...] = jnp.max(top, axis=0, keepdims=True)

    def weigh_all(couple, score_ref, top_ref, value_step):
        block, head = place(couple)
        a, b = pair_ids(couple)
        count = live(couple)
        top = top_ref[...]
        total = jnp.zeros((8, lanes), jnp.float32)
        parts = []
        for n in range(SLOTS):
            shift = top if n == 0 else jnp.where(n < count, top, -LOW)
            weights = jnp.exp2((score_ref[n * BLK : (n + 1) * BLK, :] - shift) * EXP2_SCALE)
            total += weights.reshape(16, 8, lanes).sum(0)
            parts.append(weights.astype(jnp.bfloat16))
        rounded = jnp.concatenate(parts, 0)
        row_total = jnp.sum(total, axis=0, keepdims=True)
        rows = pl.ds(pl.multiple_of(block * BLK, BLK), BLK)
        for side, pair in enumerate((a, b)):
            values = jnp.concatenate(
                [table_ref[lists[pair * SLOTS + n] + value_step] for n in range(SLOTS)], 1
            )
            mine = slice(side * BLK, (side + 1) * BLK)
            summed = jnp.dot(values, rounded[:, mine], preferred_element_type=jnp.float32)
            attended = (summed / row_total[:, mine]).T.astype(jnp.bfloat16)
            cols = pl.ds(pl.multiple_of((head + side) * BLK, BLK), BLK)
            out_ref[rows, cols] = attended

    value_step = kv_ratio
    score_all(0, score_a, top_a)

    def step(index, carry):
        first = 2 * index
        score_all(first + 1, score_b, top_b)
        weigh_all(first, score_a, top_a, value_step)
        score_all(jnp.minimum(first + 2, couple_total - 1), score_a, top_a)
        weigh_all(first + 1, score_b, top_b, value_step)
        return carry

    lax.fori_loop(0, couple_total // 2, step, 0)


def attend(lists, counts, queries, table, value_step):
    head_count, rows, width = queries.shape
    block_count = rows // BLK

    def kernel(*refs):
        attention_kernel(head_count, block_count, value_step, *refs)

    whole = pl.BlockSpec(memory_space=pltpu.VMEM)
    return pl.pallas_call(
        kernel,
        name="attend",
        grid_spec=pltpu.PrefetchScalarGridSpec(
            num_scalar_prefetch=2,
            grid=(1,),
            in_specs=[whole, whole],
            out_specs=whole,
            scratch_shapes=[pltpu.VMEM((SLOTS * BLK, 2 * BLK), jnp.float32)] * 2
            + [pltpu.VMEM((1, 2 * BLK), jnp.float32)] * 2,
        ),
        out_shape=jax.ShapeDtypeStruct((rows, head_count * width), jnp.bfloat16),
        compiler_params=pltpu.CompilerParams(vmem_limit_bytes=56 * 2**20),
    )(lists, counts, queries, table)


def body(query_states, key_states, value_states, tile_keys, tile_count, out_weight):
    head_group, row_count, width = query_states.shape
    kv_group = key_states.shape[0]
    blocks = row_count // BLK
    seq_place = lax.axis_index("seq")
    key_tiles = key_states.reshape(kv_group, blocks, BLK, width)
    value_tiles = jnp.swapaxes(value_states.reshape(kv_group, blocks, BLK, width), 2, 3)
    local = jnp.stack([key_tiles, value_tiles])
    gathered = lax.all_gather(local, "seq", axis=0, tiled=False)
    table = gathered.reshape(-1, BLK, width)
    per_shard = 2 * kv_group * blocks
    lists = lax.dynamic_slice_in_dim(tile_keys, seq_place * blocks, blocks, 1)
    counts = lax.dynamic_slice_in_dim(tile_count, seq_place * blocks, blocks, 1)
    kv_of = jnp.arange(head_group, dtype=jnp.int32) // (head_group // kv_group)
    lists = (lists // blocks) * per_shard + kv_of[:, None, None] * blocks + lists % blocks
    attended = attend(
        lists.reshape(-1), counts.reshape(-1), query_states, table, kv_group * blocks
    )
    partial = jnp.dot(attended, out_weight, preferred_element_type=jnp.float32)
    return lax.psum_scatter(
        partial.astype(jnp.bfloat16), "grp", scatter_dimension=0, tiled=True
    )


def solution(mesh):
    placed = (
        P("grp", "seq", None),
        P("grp", "seq", None),
        P("grp", "seq", None),
        P("grp", None, None),
        P("grp", None),
        P("grp", None),
    )
    return jax.shard_map(
        body, mesh=mesh, in_specs=placed, out_specs=P(("seq", "grp"), None), check_vma=False
    )
```

time: 827 us -> 188 us (0.23)
  local copies, waits for them, and re-layouts: 392 us -> 3.56 us
  other arithmetic: 137 us -> 1.89 us
  matrix products: 78 us -> 14.4 us
  waiting for transfers between devices: 158 us -> 120 us
  Pallas kernels: 0 us -> 34.7 us
  blocking collectives: 33.8 us -> 0 us
  starting transfers between devices: 9.71 us -> 0.04 us
    gather x26 -> x0, local copies, waits for them, and re-layouts: 229 us -> none  [the longest x8 92 us: attend_tiles(): jnp.take(value_table, table_rows, axis=0)]
    reshape x16 -> x3, local copies, waits for them, and re-layouts: 118 us -> 2.51 us  [the longest x1 1.15 us: body(): value_states.reshape(kv_group, blocks, BLK, width)]
    dot_general x17 -> x1, matrix products: 78 us -> 14.4 us  [body(): partial = jnp.dot(attended, out_weight, preferred_element_type=jnp.float32)]
    select_n x41 -> x0, other arithmetic: 60 us -> none  [the longest x16 59.8 us: attend_tiles(): jnp.take(key_table, table_rows, axis=0)]
    unnamed x1 -> x0, other arithmetic: 45.2 us -> none
    pallas_call x0 -> x1, Pallas kernels: none -> 34.7 us  [attend(): pl.pallas_call(kernel, name='attend', grid_spec=pltpu.PrefetchScalarGridS...]
    all_to_all x1 -> x0, blocking collectives: 33.8 us -> none  [body(): lax.all_to_all(attended.reshape(unit_count, seq_total // 2, head_width),...]
    reduce_scatter x1, waiting for transfers between devices: 78 us -> 46 us  [body(): lax.psum_scatter(partial.astype(jnp.bfloat16), 'grp', scatter_dimension=0...]
  transfers between devices with their start and end apart: 3 -> 2, of which waited for: 2 -> 2; matrix products, arithmetic and copies ran while one was open for 3% -> 1% of each run, Pallas kernels for 0% -> 0%
where the time goes in v1:
time: 188 us
  waiting for transfers between devices  120 us (64%)
  Pallas kernels  34.7 us (18%)
  matrix products  14.4 us (8%)
  between operations  13.4 us (7%)
  local copies, waits for them, and re-layouts  3.56 us (2%)
  other arithmetic  1.89 us (1%)
    all_gather x1, waiting for transfers between devices, body(): gathered = lax.all_gather(local, 'seq', axis=0, tiled=False)  73.8 us
    reduce_scatter x1, waiting for transfers between devices, body(): lax.psum_scatter(partial.astype(jnp.bfloat16), 'grp', scatter_dimension=0...  46 us
    pallas_call x1, Pallas kernels, attend(): pl.pallas_call(kernel, name='attend', grid_spec=pltpu.PrefetchScalarGridS...  34.7 us
    dot_general x1, matrix products, body(): partial = jnp.dot(attended, out_weight, preferred_element_type=jnp.float32)  14.4 us
  transfers between devices with their start and end apart: 2, of which 2 were waited for; matrix products, arithmetic and copies ran while one was open for 1% of the time, Pallas kernels for 0%

profile of v1, /device:TPU:1, one launch (start us, length us, event | category | flops | bytes accessed | tf_op | source)
XLA Modules:
  0.0 187.9 jit_solution(2175268753346739010)
XLA Ops:
  6.5 0.0 copy-start
  6.5 0.0 all-gather.3.cloned.1.call-start
  6.5 1.2 copy.17
  7.7 1.8 pad_maximum_fusion
  9.5 0.0 all-gather.3.cloned.1.call-update
  9.5 0.0 reduce-scatter.2.cloned.1.call-start
  9.6 0.8 constant_dynamic-slice_fusion
  10.3 0.7 reshape.28.refs_1_
  11.0 0.0 copy-done
  11.0 0.1 constant_dynamic-slice_fusion.1
  11.1 0.2 copy.18
  11.3 0.1 fusion.2
  11.4 0.7 reshape.27.refs_0_
  12.1 73.8 %all-gather.3.cloned.1.call-done = bf16[64,2,4,128,128]{4,3,2,1,0:T(8,128)(2,1)} async-done(((bf16[2,2,4,128,128]{4,3,2,1,0:T(8,128)(2,1)}), bf16[64,2,4,128,128]{4,3,2,1,0:T(8,128)(2,1)}) %all-gather.3.cloned.1.call-update) | async-done | bytes 16777232 | tf_op jit(solution)/shard_map/all_gather | solution.py:139
  85.9 34.7 %attend.1 = bf16[512,2048]{1,0:T(8,128)(2,1)} custom-call(s32[1024]{0:T(1024)} %reshape.27.refs_0_, s32[64]{0:T(128)} %reshape.28.refs_1_, bf16[16,512,128]{2,1,0:T(8,128)(2,1)} %refs_2_.1, bf16[512,128,128]{2,1,0:T(8,128)(2,1)} %bitcast.8), custom_call_target="tpu_custom_call" | custom-call | tf_op jit(solution)/shard_map/attend/pallas_call | solution.py:115
  120.7 14.4 %convolution_convert_fusion = bf16[512,4096]{1,0:T(8,128)(2,1)} fusion(bf16[512,2048]{1,0:T(8,128)(2,1)} %attend.1, bf16[2048,4096]{1,0:T(8,128)(2,1)} %param.11), kind=kOutput, calls=%fused_computation | convolution fusion | flops 8592031744 | bytes 23068672 | tf_op jit(solution)/shard_map/dot_general | solution.py:149
  135.1 0.0 reduce-scatter.2.cloned.1.call-update
  135.1 46.0 %reduce-scatter.2.cloned.1.call-done = bf16[128,4096]{1,0:T(8,128)(2,1)} async-done(((bf16[512,4096]{1,0:T(8,128)(2,1)}), bf16[128,4096]{1,0:T(8,128)(2,1)}) %reduce-scatter.2.cloned.1.call-update) | async-done | bytes 1048592 | tf_op jit(solution)/shard_map/reduce_scatter | solution.py:150
  (2 shorter events, 0.0 us)
Async XLA Ops:
  6.5 4.5 %copy-start = (s32[16,128,16]{1,2,0:T(8,128)S(1)}, s32[16,128,16]{1,2,0:T(8,128)}, u32[]{:S(2)}) copy-start(s32[16,128,16]{1,2,0:T(8,128)} %param.9) | copy-start | bytes 393220
  6.5 79.4 %all-gather.3.cloned.1.call-start = ((), (), s32[]{:S(2)}) async-start(), calls=%async_computation.2 | async-start | bytes 17301504 | tf_op jit(solution)/shard_map/all_gather | solution.py:139
  9.5 171.5 %reduce-scatter.2.cloned.1.call-start = ((), (), s32[]{:S(2)}) async-start(), calls=%async_computation.1 | async-start | bytes 5242880 | tf_op jit(solution)/shard_map/reduce_scatter | solution.py:150
Sparse Core Ops, SparseCore 0:
  9.6 76.2 all-gather.2
  135.2 45.7 reduce-scatter.1

commit v2 on v1

v2 whole, which is shorter than its diff:
```python
import functools
import math

import jax
import jax.numpy as jnp
from jax import lax
from jax.experimental import pallas as pl
from jax.experimental.pallas import tpu as pltpu
from jax.sharding import PartitionSpec as P

BLK = 128
SLOTS = 16
PAIR = 2 * BLK
SPAN = SLOTS * BLK
RING = 4
CORES = 2
SEQ_DEVICES = RING * RING * CORES
CHUNK_COUPLES = 8
EXP2_SCALE = float(BLK ** -0.5 * math.log2(math.e))
LOW = -1e30
LIMIT = 16 * 2**20

VMEM = pl.BlockSpec(memory_space=pltpu.VMEM)
HBM = pl.BlockSpec(memory_space=pltpu.HBM)


def cat(parts, axis):
    return jnp.concatenate(parts, axis)


def score_kernel(first, groups, lists, counts, place, q_ref, *refs):
    pieces, refs = refs[:10], refs[10:]
    weight_refs, total_ref, refs = refs[:groups], refs[groups], refs[groups + 1 :]
    score_a, score_b, top_a, top_b, table, sems = refs
    key_row = lax.broadcasted_iota(jnp.int32, (BLK, PAIR), 0)
    query_row = lax.broadcasted_iota(jnp.int32, (BLK, PAIR), 1) % BLK
    lane = lax.broadcasted_iota(jnp.int32, (1, PAIR), 1)
    zero = jnp.zeros((BLK, BLK), jnp.bfloat16)
    last = first + groups * CHUNK_COUPLES - 1

    copies, at = [], 0
    for index, piece in enumerate(pieces):
        size = piece.shape[0]
        copies.append(
            pltpu.make_async_copy(piece, table.at[pl.ds(at, size)], sems.at[index])
        )
        at += size
    for copy in copies:
        copy.start()
    for copy in copies:
        copy.wait()

    def live(couple):
        return jnp.where(lane < BLK, counts[2 * couple], counts[2 * couple + 1])

    def score(couple, score_ref, top_ref):
        chunk = couple // CHUNK_COUPLES
        side = (couple // 4) % 2
        head = 2 * (couple % 4)
        rows = pl.ds(pl.multiple_of(place[1 + chunk] * BLK, BLK), BLK)
        qa = q_ref[side, head, rows, :].T
        qb = q_ref[side, head + 1, rows, :].T
        queries = cat([cat([qa, zero], 1), cat([zero, qb], 1)], 0)
        a = 2 * couple * SLOTS
        keys = cat(
            [cat([table[lists[a + n]], table[lists[a + SLOTS + n]]], 1) for n in range(SLOTS)], 0
        )
        scores = jnp.dot(keys, queries, preferred_element_type=jnp.float32)
        count = live(couple)
        top = None
        for n in range(SLOTS):
            tile = scores[n * BLK : (n + 1) * BLK]
            if n == 0:
                tile = jnp.where(key_row <= query_row, tile, LOW)
                top = tile.reshape(16, 8, PAIR).max(0)
            else:
                best = tile.reshape(16, 8, PAIR).max(0)
                top = jnp.maximum(top, jnp.where(n < count, best, LOW))
            score_ref[n * BLK : (n + 1) * BLK, :] = tile
        top_ref[...] = jnp.max(top, axis=0, keepdims=True)

    def weigh(couple, slot, weight_ref, score_ref, top_ref):
        count = live(couple)
        top = top_ref[...]
        total = jnp.zeros((8, PAIR), jnp.float32)
        for n in range(SLOTS):
            shift = top if n == 0 else jnp.where(n < count, top, -LOW)
            weights = jnp.exp2((score_ref[n * BLK : (n + 1) * BLK, :] - shift) * EXP2_SCALE)
            total += weights.reshape(16, 8, PAIR).sum(0)
            weight_ref[slot, n * BLK : (n + 1) * BLK, :] = weights.astype(jnp.bfloat16)
        total_ref[couple - first] = jnp.sum(total, axis=0, keepdims=True)

    score(first, score_a, top_a)
    for group in range(groups):
        base = first + group * CHUNK_COUPLES

        def step(index, carry, base=base, weight_ref=weight_refs[group]):
            couple = base + 2 * index
            score(couple + 1, score_b, top_b)
            weigh(couple, 2 * index, weight_ref, score_a, top_a)
            score(jnp.minimum(couple + 2, last), score_a, top_a)
            weigh(couple + 1, 2 * index + 1, weight_ref, score_b, top_b)
            return carry

        lax.fori_loop(0, CHUNK_COUPLES // 2, step, 0)


def score_call(name, first, groups, lists, counts, place, queries, pieces):
    couples = groups * CHUNK_COUPLES
    return pl.pallas_call(
        functools.partial(score_kernel, first, groups),
        name=name,
        grid_spec=pltpu.PrefetchScalarGridSpec(
            num_scalar_prefetch=3,
            grid=(1,),
            in_specs=[VMEM] + [HBM] * len(pieces),
            out_specs=[VMEM] * (groups + 1),
            scratch_shapes=[pltpu.VMEM((SPAN, PAIR), jnp.float32)] * 2
            + [pltpu.VMEM((1, PAIR), jnp.float32)] * 2
            + [
                pltpu.VMEM((BLK, BLK, BLK), jnp.bfloat16),
                pltpu.SemaphoreType.DMA((len(pieces),)),
            ],
        ),
        out_shape=[pltpu.VMEM((CHUNK_COUPLES, SPAN, PAIR), jnp.bfloat16)] * groups
        + [jax.ShapeDtypeStruct((couples, 1, PAIR), jnp.float32)],
        compiler_params=pltpu.CompilerParams(vmem_limit_bytes=LIMIT),
        cost_estimate=pl.CostEstimate(
            flops=couples * 2 * SPAN * PAIR * PAIR,
            bytes_accessed=couples * SPAN * PAIR * 2,
            transcendentals=couples * SPAN * PAIR,
        ),
    )(lists, counts, place, queries, *pieces)


def combine(couple, slot, group, lists, weight_ref, total, values_ref, out_ref):
    head = 2 * (couple % 4)
    for side in range(2):
        pair = 2 * couple + side
        values = cat([values_ref[lists[pair * SLOTS + n]] for n in range(SLOTS)], 1)
        mine = slice(side * BLK, (side + 1) * BLK)
        summed = jnp.dot(values, weight_ref[slot, :, mine], preferred_element_type=jnp.float32)
        attended = (summed / total[:, mine]).T.astype(jnp.bfloat16)
        cols = pl.ds(pl.multiple_of((head + side) * BLK, BLK), BLK)
        rows = slice(group * BLK, (group + 1) * BLK)
        which = (couple // 4) % 2
        out_ref[which, rows, cols] = attended


def combine_loop(first, group, lists, weight_ref, total_ref, total_first, values_ref, out_ref):
    def step(index, carry):
        for k in range(4):
            slot = 4 * index + k
            couple = first + group * CHUNK_COUPLES + slot
            combine(
                couple,
                slot,
                group,
                lists,
                weight_ref,
                total_ref[couple - total_first],
                values_ref,
                out_ref,
            )
        return carry

    lax.fori_loop(0, CHUNK_COUPLES // 4, step, 0)


def first_values_kernel(lists, place, weight_ref, total_ref, gathered_ref, out_ref, values_ref, sem):
    copy = pltpu.make_async_copy(gathered_ref.at[:, place[0]], values_ref, sem)
    copy.start()
    copy.wait()
    values = values_ref.reshape(BLK, BLK, BLK)
    combine_loop(0, 0, lists, weight_ref, total_ref, 0, values, out_ref)


def first_values_call(lists, place, weights, totals, gathered):
    shards, _, tiles = gathered.shape[:3]
    return pl.pallas_call(
        first_values_kernel,
        name="values_first",
        grid_spec=pltpu.PrefetchScalarGridSpec(
            num_scalar_prefetch=2,
            grid=(1,),
            in_specs=[VMEM, VMEM, HBM],
            out_specs=[VMEM, VMEM],
            scratch_shapes=[pltpu.SemaphoreType.DMA],
        ),
        out_shape=[
            jax.ShapeDtypeStruct((2, BLK, 8 * BLK), jnp.bfloat16),
            pltpu.VMEM((shards, tiles, BLK, BLK), jnp.bfloat16),
        ],
        compiler_params=pltpu.CompilerParams(vmem_limit_bytes=LIMIT),
        cost_estimate=pl.CostEstimate(
            flops=CHUNK_COUPLES * 2 * SPAN * PAIR * BLK,
            bytes_accessed=CHUNK_COUPLES * SPAN * PAIR * 2,
            transcendentals=0,
        ),
    )(lists, place, weights, totals, gathered)


def next_values_kernel(
    first, total_first, groups, with_weight, lists, total_ref, values_ref, after_ref, *refs
):
    weight_refs, refs = refs[:groups], refs[groups:]
    if with_weight:
        proj_ref, out_ref, held_ref, sem = refs
        copy = pltpu.make_async_copy(proj_ref, held_ref, sem)
        copy.start()
    else:
        (out_ref,) = refs
    values = values_ref.reshape(BLK, BLK, BLK)
    for group in range(groups):
        combine_loop(
            first, group, lists, weight_refs[group], total_ref, total_first, values, out_ref
        )
    if with_weight:
        copy.wait()


def next_values_call(name, first, total_first, lists, totals, values, after, weights, proj=None):
    groups = len(weights)
    with_weight = proj is not None
    out_shape = [jax.ShapeDtypeStruct((2, groups * BLK, 8 * BLK), jnp.bfloat16)]
    if with_weight:
        out_shape.append(pltpu.VMEM(proj.shape, proj.dtype))
    return pl.pallas_call(
        functools.partial(next_values_kernel, first, total_first, groups, with_weight),
        name=name,
        grid_spec=pltpu.PrefetchScalarGridSpec(
            num_scalar_prefetch=1,
            grid=(1,),
            in_specs=[VMEM, VMEM, HBM] + [VMEM] * groups + [HBM] * with_weight,
            out_specs=[VMEM] * len(out_shape),
            scratch_shapes=[pltpu.SemaphoreType.DMA] * with_weight,
        ),
        out_shape=out_shape,
        compiler_params=pltpu.CompilerParams(vmem_limit_bytes=LIMIT),
        cost_estimate=pl.CostEstimate(
            flops=groups * CHUNK_COUPLES * 2 * SPAN * PAIR * BLK,
            bytes_accessed=groups * CHUNK_COUPLES * SPAN * PAIR * 2,
            transcendentals=0,
        ),
    )(lists, totals, values, after, *weights, *((proj,) if with_weight else ()))


def project_kernel(kind, place, mine_ref, theirs_ref, held_ref, *refs):
    rows = mine_ref.shape[0]
    depth = mine_ref.shape[1]
    width = held_ref.shape[1]
    tile = 1024
    core = place[0]
    mine = mine_ref[...]
    theirs = theirs_ref[...]
    left = jnp.where(core == 0, mine, theirs)
    right = jnp.where(core == 0, theirs, mine)
    both = cat([left, right], 1)
    for at in range(0, width, tile):
        cols = slice(at, at + tile)
        total = jnp.dot(both, held_ref[:, cols], preferred_element_type=jnp.float32)
        if kind == "far":
            low_ref, high_ref = refs
            if at < width // 2:
                low_ref[:, cols] = total.astype(jnp.bfloat16)
            else:
                high_ref[:, at - width // 2 : at - width // 2 + tile] = total.astype(jnp.bfloat16)
        elif kind == "near":
            low_in, high_in, up_ref, down_ref = refs
            up = total[:BLK]
            down = total[BLK:]
            if at < width // 2:
                up = up + low_in[:, cols].astype(jnp.float32)
            else:
                start = at - width // 2
                down = down + high_in[:, start : start + tile].astype(jnp.float32)
            up_ref[:, cols] = up.astype(jnp.bfloat16)
            down_ref[:, cols] = down.astype(jnp.bfloat16)
        else:
            (out_ref,) = refs
            out_ref[:, cols] = total


def project_call(kind, place, mine, theirs, held, *arrived):
    width = held.shape[1]
    shapes = {
        "far": [((BLK, width // 2), jnp.bfloat16)] * 2,
        "near": [((BLK, width), jnp.bfloat16)] * 2,
        "own": [((BLK, width), jnp.float32)],
    }[kind]
    rows = mine.shape[0]
    return pl.pallas_call(
        functools.partial(project_kernel, kind),
        name="project_" + kind,
        grid_spec=pltpu.PrefetchScalarGridSpec(
            num_scalar_prefetch=1,
            grid=(1,),
            in_specs=[VMEM] * (3 + len(arrived)),
            out_specs=[VMEM] * len(shapes),
        ),
        out_shape=[jax.ShapeDtypeStruct(*shape) for shape in shapes],
        compiler_params=pltpu.CompilerParams(vmem_limit_bytes=LIMIT),
        cost_estimate=pl.CostEstimate(
            flops=2 * rows * held.shape[0] * width,
            bytes_accessed=held.shape[0] * width * 2,
            transcendentals=0,
        ),
    )(place, mine, theirs, held, *arrived)


def chip_perm(phase, step):
    pairs = []
    for z in range(RING):
        for y in range(RING):
            for core in range(CORES):
                if (core == 0) == (phase == 0):
                    to_z, to_y = z, (y + step) % RING
                else:
                    to_z, to_y = (z + step) % RING, y
                pairs.append(((z * RING + y) * CORES + core, (to_z * RING + to_y) * CORES + core))
    return pairs


SWAP = [(i, i ^ 1) for i in range(SEQ_DEVICES)]


def along(array, phase, step):
    return lax.ppermute(array, "seq", chip_perm(phase, step))


def swap(array):
    return lax.ppermute(array, "seq", SWAP)


def turn(array, step):
    return lax.ppermute(array, "grp", [(i, (i + step) % RING) for i in range(RING)])


def gather_keys(own):
    left, right = along(own, 0, 1), along(own, 0, -1)
    far = along(own, 0, 2)
    low, high = cat([own, left], 0), cat([right, far], 0)
    left_low, right_high = along(low, 1, 1), along(high, 1, -1)
    left_high, right_low = along(high, 1, 1), along(low, 1, -1)
    far_low, far_high = along(left_low, 1, 1), along(right_high, 1, -1)
    return [own, left, right, far, left_low, left_high, right_low, right_high, far_low, far_high]


def body(query_states, key_states, value_states, tile_keys, tile_count, out_weight):
    head_group, row_count, width = query_states.shape
    kv_group = key_states.shape[0]
    blocks = row_count // BLK
    heads = head_group // kv_group
    seq_place = lax.axis_index("seq")
    grp_place = lax.axis_index("grp")
    core = seq_place % CORES
    chip = seq_place // CORES
    chip_z, chip_y = chip // RING, chip % RING

    value_tiles = jnp.swapaxes(value_states.reshape(kv_group, blocks, BLK, width), 2, 3)
    gathered = lax.all_gather(value_tiles, "seq", axis=0, tiled=False)

    key_tiles = key_states.reshape(kv_group, blocks, BLK, width)
    own_keys = cat(
        [
            lax.dynamic_index_in_dim(key_tiles, core, 0, keepdims=False),
            swap(lax.dynamic_index_in_dim(key_tiles, 1 - core, 0, keepdims=False)),
        ],
        0,
    )
    pieces = gather_keys(own_keys)

    queries = jnp.stack(
        [
            swap(lax.dynamic_slice_in_dim(query_states, (1 - core) * heads, heads, 0)),
            lax.dynamic_slice_in_dim(query_states, core * heads, heads, 0),
        ]
    )

    chunks = (grp_place + jnp.array([2, 1, 3, 0], jnp.int32)) % RING
    place = jnp.concatenate([core[None], chunks]).astype(jnp.int32)
    sides = jnp.stack([1 - core, core])
    order = (chip * 2 * blocks + sides[None, :] * blocks + chunks[:, None]).reshape(-1)
    my_lists = lax.dynamic_slice_in_dim(tile_keys, core * heads, heads, 0)
    my_counts = lax.dynamic_slice_in_dim(tile_count, core * heads, heads, 0)
    value_lists = jnp.swapaxes(jnp.take(my_lists, order, axis=1), 0, 1)
    counts = jnp.swapaxes(jnp.take(my_counts, order, axis=1), 0, 1).reshape(-1)

    span = 2 * blocks
    from_chip = value_lists // span
    inside = value_lists % span
    step_z = (from_chip // RING - chip_z) % RING
    step_y = (from_chip % RING - chip_y) % RING

    def arrival(step):
        return jnp.where(step == 1, 2, jnp.where(step == 2, 3, jnp.where(step == 3, 1, 0)))

    inner = arrival(jnp.where(core == 0, step_y, step_z))
    outer = arrival(jnp.where(core == 0, step_z, step_y))
    key_lists = (
        (outer * RING + inner) * span
        + (inside // blocks + core) % CORES * blocks
        + inside % blocks
    )
    key_lists = key_lists.reshape(-1)
    value_lists = value_lists.reshape(-1)

    far_w, up_w, down_w, totals = score_call(
        "scores", 0, 3, key_lists, counts, place, queries, pieces
    )
    far_att, values = first_values_call(value_lists, place, far_w, totals, gathered)
    near_att, held = next_values_call(
        "values_near",
        CHUNK_COUPLES,
        0,
        value_lists,
        totals,
        values,
        far_att,
        [up_w, down_w],
        out_weight,
    )
    low, high = project_call("far", place, far_att[1], swap(far_att[0]), held)
    low_in, high_in = turn(low, 1), turn(high, -1)
    own_w, own_totals = score_call(
        "scores_own", 3 * CHUNK_COUPLES, 1, key_lists, counts, place, queries, pieces
    )
    up, down = project_call(
        "near", place, near_att[1], swap(near_att[0]), held, low_in, high_in
    )
    from_left, from_right = turn(up, 1), turn(down, -1)
    (own_att,) = next_values_call(
        "values_own",
        3 * CHUNK_COUPLES,
        3 * CHUNK_COUPLES,
        value_lists,
        own_totals,
        values,
        near_att,
        [own_w],
    )
    (own,) = project_call("own", place, own_att[1], swap(own_att[0]), held)
    total = own + from_left.astype(jnp.float32) + from_right.astype(jnp.float32)
    return total.astype(jnp.bfloat16)


def solution(mesh):
    placed = (
        P("grp", "seq", None),
        P("grp", "seq", None),
        P("grp", "seq", None),
        P("grp", None, None),
        P("grp", None),
        P("grp", None),
    )
    return jax.shard_map(
        body, mesh=mesh, in_specs=placed, out_specs=P(("seq", "grp"), None), check_vma=False
    )
```

time: 188 us -> 178 us (0.947)
  waiting for transfers between devices: 120 us -> 42.9 us
  local copies, waits for them, and re-layouts: 3.56 us -> 38 us
  starting transfers between devices: 0.04 us -> 28.8 us
  Pallas kernels: 34.7 us -> 49.3 us
  matrix products: 14.4 us -> 0 us
  other arithmetic: 1.89 us -> 4.51 us
    all_gather x1, waiting for transfers between devices: 73.8 us -> 0.01 us  [body(): gathered = lax.all_gather(value_tiles, 'seq', axis=0, tiled=False)]
    reduce_scatter x1 -> x0, waiting for transfers between devices: 46 us -> none  [body(): lax.psum_scatter(partial.astype(jnp.bfloat16), 'grp', scatter_dimension=0...]
    ppermute x0 -> x18, waiting for transfers between devices: none -> 42.9 us  [the longest x9 28.3 us: along(): return lax.ppermute(array, 'seq', chip_perm(phase, step))]
    unnamed x3 -> x31, local copies, waits for them, and re-layouts: 0.17 us -> 31.1 us
    ppermute x0 -> x18, starting transfers between devices: none -> 28.7 us  [the longest x9 13.1 us: along(): return lax.ppermute(array, 'seq', chip_perm(phase, step))]
    pallas_call x1 -> x8, Pallas kernels: 34.7 us -> 49.3 us  [the longest x2 25.1 us: score_call(): pl.pallas_call(functools.partial(score_kernel, first, groups), name=name,...]
    dot_general x1 -> x0, matrix products: 14.4 us -> none  [body(): partial = jnp.dot(attended, out_weight, preferred_element_type=jnp.float32)]
    reshape x3, local copies, waits for them, and re-layouts: 2.51 us -> 0.23 us  [the longest x1 0.08 us: body(): counts = jnp.swapaxes(jnp.take(my_counts, order, axis=1), 0, 1).reshape(-1)]
  transfers between devices with their start and end apart: 2 -> 19, of which waited for: 2 -> 9; matrix products, arithmetic and copies ran while one was open for 1% -> 5% of each run, Pallas kernels for 0% -> 23%
where the time goes in v2:
time: 178 us; the launch traced here: 177 us
  Pallas kernels  49.3 us (28%)
  waiting for transfers between devices  42.9 us (24%)
  local copies, waits for them, and re-layouts  38 us (21%)
  starting transfers between devices  28.8 us (16%)
  between operations  13.7 us (8%)
  other arithmetic  4.51 us (3%)
    unnamed x31, local copies, waits for them, and re-layouts  31.1 us
    ppermute x9, waiting for transfers between devices, along(): return lax.ppermute(array, 'seq', chip_perm(phase, step))  28.3 us
    pallas_call x2, Pallas kernels, score_call(): pl.pallas_call(functools.partial(score_kernel, first, groups), name=name,...  25.1 us
    ppermute x9, starting transfers between devices, along(): return lax.ppermute(array, 'seq', chip_perm(phase, step))  13.1 us
    ppermute x4, waiting for transfers between devices, turn(): lax.ppermute(array, 'grp', [(i, (i + step) % RING) for i in range(RING)])  11.5 us
    pallas_call x3, Pallas kernels, project_call(): pl.pallas_call(functools.partial(project_kernel, kind), name='project_' +...  10.8 us
    ppermute x5, starting transfers between devices, swap(): return lax.ppermute(array, 'seq', SWAP)  9.96 us
    pallas_call x2, Pallas kernels, next_values_call(): pl.pallas_call(functools.partial(next_values_kernel, first, total_first,...  9.65 us
  transfers between devices with their start and end apart: 19, of which 9 were waited for; matrix products, arithmetic and copies ran while one was open for 5% of the time, Pallas kernels for 23%

profile of v2, /device:TPU:1, one launch (start us, length us, event | category | flops | bytes accessed | tf_op | source)
XLA Modules:
  0.0 177.2 jit_solution(754119947811542079)
XLA Ops:
  6.5 1.8 %copy.17 = bf16[2,4,128,128]{3,2,1,0:T(8,128)(2,1)} copy(bf16[2,4,128,128]{2,3,1,0:T(8,128)(2,1)} %bitcast.29) | data formatting | bytes 524288 | tf_op jit(solution)/shard_map/transpose | solution.py:360
  8.4 2.7 %constant_dynamic-slice_fusion = (bf16[8,512,128]{2,1,0:T(8,128)(2,1)S(1)}, bf16[1,8,512,128]{3,2,1,0:T(8,128)(2,1)}) fusion(bf16[16,512,128]{2,1,0:T(8,128)(2,1)} %param.7, s32[]{:T(128)S(6)} %select_n.172, s32[]{:T(128)S(6)} %select_n.146), kind=kLoop, calls=%fused_computation.66 | loop fusion | bytes 4194312 | tf_op jit(solution)/shard_map/dynamic_slice | solution.py:375
  13.0 2.0 %collective-permute-done.1 = bf16[4,128,128]{2,1,0:T(8,128)(2,1)S(1)} collective-permute-done((bf16[4,128,128]{2,1,0:T(8,128)(2,1)S(1)}, bf16[4,128,128]{2,1,0:T(8,128)(2,1)S(1)}, u32[]{:S(2)}, u32[]{:S(2)}) %collective-permute-start.1) | collective-permute-done | bytes 131104 | tf_op jit(solution)/shard_map/ppermute | solution.py:332
  15.0 3.9 %collective-permute-start.3 = (bf16[8,128,128]{2,1,0:T(8,128)(2,1)S(1)}, bf16[8,128,128]{2,1,0:T(8,128)(2,1)S(1)}, u32[]{:S(2)}, u32[]{:S(2)}) collective-permute-start(bf16[8,128,128]{2,1,0:T(8,128)(2,1)S(1)} %pad_maximum_fusion.2.refs_0_), channel_id=1, source_target_pairs={{0,24},{4,100},{8,0},{12,108},{16,8},{20,116},{24,16},{28,124},{32... | collective-permute-start | bytes 786440 | tf_op jit(solution)/shard_map/ppermute | solution.py:328
  20.0 6.5 %collective-permute-done.3.refs_2_ = bf16[8,128,128]{2,1,0:T(8,128)(2,1)S(1)} collective-permute-done((bf16[8,128,128]{2,1,0:T(8,128)(2,1)S(1)}, bf16[8,128,128]{2,1,0:T(8,128)(2,1)S(1)}, u32[]{:S(2)}, u32[]{:S(2)}) %collective-permute-start.3) | collective-permute-done | bytes 262176 | tf_op jit(solution)/shard_map/ppermute | solution.py:328
  27.9 2.7 %collective-permute-start.8 = (bf16[16,128,128]{2,1,0:T(8,128)(2,1)}, bf16[16,128,128]{2,1,0:T(8,128)(2,1)}, u32[]{:S(2)}, u32[]{:S(2)}) collective-permute-start(bf16[16,128,128]{2,1,0:T(8,128)(2,1)} %constant_dynamic-update-slice_fusion), channel_id=1, source_target_pairs={{0,96},{4,28},{8,104},{12,4},{16,112},{20,12},{24,120},{28,20},{32... | collective-permute-start | bytes 1572872 | tf_op jit(solution)/shard_map/ppermute | solution.py:328
  35.3 3.6 %collective-permute-done.8.refs_7_ = bf16[16,128,128]{2,1,0:T(8,128)(2,1)} collective-permute-done((bf16[16,128,128]{2,1,0:T(8,128)(2,1)}, bf16[16,128,128]{2,1,0:T(8,128)(2,1)}, u32[]{:S(2)}, u32[]{:S(2)}) %collective-permute-start.8) | collective-permute-done | bytes 524320 | tf_op jit(solution)/shard_map/ppermute | solution.py:328
  39.0 2.8 %collective-permute-start.10 = (bf16[16,128,128]{2,1,0:T(8,128)(2,1)}, bf16[16,128,128]{2,1,0:T(8,128)(2,1)}, u32[]{:S(2)}, u32[]{:S(2)}) collective-permute-start(bf16[16,128,128]{2,1,0:T(8,128)(2,1)} %collective-permute-done.8.refs_7_), channel_id=1, source_target_pairs={{0,96},{4,28},{8,104},{12,4},{16,112},{20,12},{24,120},{28,20},{32... | collective-permute-start | bytes 1572872 | tf_op jit(solution)/shard_map/ppermute | solution.py:328
  44.9 2.8 %collective-permute-done.6.refs_5_ = bf16[16,128,128]{2,1,0:T(8,128)(2,1)} collective-permute-done((bf16[16,128,128]{2,1,0:T(8,128)(2,1)}, bf16[16,128,128]{2,1,0:T(8,128)(2,1)}, u32[]{:S(2)}, u32[]{:S(2)}) %collective-permute-start.6) | collective-permute-done | bytes 524320 | tf_op jit(solution)/shard_map/ppermute | solution.py:328
  47.7 10.6 %collective-permute-done.10.refs_9_ = bf16[16,128,128]{2,1,0:T(8,128)(2,1)} collective-permute-done((bf16[16,128,128]{2,1,0:T(8,128)(2,1)}, bf16[16,128,128]{2,1,0:T(8,128)(2,1)}, u32[]{:S(2)}, u32[]{:S(2)}) %collective-permute-start.10) | collective-permute-done | bytes 524320 | tf_op jit(solution)/shard_map/ppermute | solution.py:328
  58.3 4.4 %collective-permute-done.9.refs_8_ = bf16[16,128,128]{2,1,0:T(8,128)(2,1)} collective-permute-done((bf16[16,128,128]{2,1,0:T(8,128)(2,1)}, bf16[16,128,128]{2,1,0:T(8,128)(2,1)}, u32[]{:S(2)}, u32[]{:S(2)}) %collective-permute-start.9) | collective-permute-done | bytes 524320 | tf_op jit(solution)/shard_map/ppermute | solution.py:328
  62.7 17.2 %scores.1 = (bf16[8,2048,256]{2,1,0:T(8,128)(2,1)S(1)}, bf16[8,2048,256]{2,1,0:T(8,128)(2,1)S(1)}, bf16[8,2048,256]{2,1,0:T(8,128)(2,1)S(1)}, f32[24,1,256]{2,1,0:T(1,128)S(1)}) custom-call(s32[1024]{0:T(1024)S(1)} %reshape.76.lists, s32[64]{0:T(128)S(1)} %reshape.77.counts, s32[5]{0:T(128)S(1)} %pad_add_fusion.place, ...), custom_call_target="tpu_custom_call" | custom-call | flops 6442450944 | bytes 25165824 | tf_op jit(solution)/shard_map/scores/pallas_call | solution.py:110
  79.9 3.2 %copy-done.2 = bf16[8,2048,256]{2,1,0:T(8,128)(2,1)} copy-done((bf16[8,2048,256]{2,1,0:T(8,128)(2,1)}, bf16[8,2048,256]{2,1,0:T(8,128)(2,1)S(1)}, u32[]{:S(2)}) %copy-start.2) | copy-done | bytes 8388632
  83.1 3.3 %copy-done.4 = bf16[8,2048,256]{2,1,0:T(8,128)(2,1)} copy-done((bf16[8,2048,256]{2,1,0:T(8,128)(2,1)}, bf16[8,2048,256]{2,1,0:T(8,128)(2,1)S(1)}, u32[]{:S(2)}) %copy-start.4) | copy-done | bytes 8388632
  86.4 3.2 %copy-done.9 = bf16[8,2048,256]{2,1,0:T(8,128)(2,1)} copy-done((bf16[8,2048,256]{2,1,0:T(8,128)(2,1)}, bf16[8,2048,256]{2,1,0:T(8,128)(2,1)S(1)}, u32[]{:S(2)}) %copy-start.9) | copy-done | bytes 8388632
  89.6 3.4 %copy-done.8 = bf16[64,4,128,128]{3,2,1,0:T(8,128)(2,1)S(1)} copy-done((bf16[64,4,128,128]{3,2,1,0:T(8,128)(2,1)S(1)}, bf16[64,4,128,128]{3,2,1,0:T(8,128)(2,1)}, u32[]{:S(2)}) %copy-start.8) | copy-done | bytes 8388632
  93.0 3.4 %copy-done.10 = bf16[8,2048,256]{2,1,0:T(8,128)(2,1)S(1)} copy-done((bf16[8,2048,256]{2,1,0:T(8,128)(2,1)S(1)}, bf16[8,2048,256]{2,1,0:T(8,128)(2,1)}, u32[]{:S(2)}) %copy-start.10) | copy-done | bytes 8388632
  96.4 3.7 %values_first.1 = (bf16[2,128,1024]{2,1,0:T(8,128)(2,1)S(1)}, bf16[32,4,128,128]{3,2,1,0:T(8,128)(2,1)S(1)}) custom-call(s32[1024]{0:T(1024)S(1)} %reshape.75.lists, s32[5]{0:T(128)S(1)} %pad_add_fusion.place, bf16[8,2048,256]{2,1,0:T(8,128)(2,1)S(1)} %copy-done.10, f32[24,1,256]{2,1,0:T(1,128)S(1)} %get-tuple-element.21.total_ref, ...), custom_call_target="tpu_custom_call" | custom-call | flops 1073741824 | bytes 8388608 | tf_op jit(solution)/shard_map/values_first/pallas_call | solution.py:180
  100.2 6.4 %collective-permute-start.13 = (bf16[128,1024]{1,0:T(8,128)(2,1)S(1)}, bf16[128,1024]{1,0:T(8,128)(2,1)S(1)}, u32[]{:S(2)}, u32[]{:S(2)}) collective-permute-start(bf16[128,1024]{1,0:T(8,128)(2,1)S(1)} %get-tuple-element.41), channel_id=1, source_target_pairs={{0,4},{4,0},{8,12},{12,8},{16,20},{20,16},{24,28},{28,24},{32,36},... | collective-permute-start | bytes 786440 | tf_op jit(solution)/shard_map/ppermute | solution.py:332
  106.6 3.4 %copy-done.3 = bf16[8,2048,256]{2,1,0:T(8,128)(2,1)S(1)} copy-done((bf16[8,2048,256]{2,1,0:T(8,128)(2,1)S(1)}, bf16[8,2048,256]{2,1,0:T(8,128)(2,1)}, u32[]{:S(2)}) %copy-start.3) | copy-done | bytes 8388632
  110.0 3.4 %copy-done.5 = bf16[8,2048,256]{2,1,0:T(8,128)(2,1)S(1)} copy-done((bf16[8,2048,256]{2,1,0:T(8,128)(2,1)S(1)}, bf16[8,2048,256]{2,1,0:T(8,128)(2,1)}, u32[]{:S(2)}) %copy-start.5) | copy-done | bytes 8388632
  113.4 6.4 %values_near.1 = (bf16[2,256,1024]{2,1,0:T(8,128)(2,1)S(1)}, bf16[2048,4096]{1,0:T(8,128)(2,1)S(1)}) custom-call(s32[1024]{0:T(1024)S(1)} %reshape.75.lists, f32[24,1,256]{2,1,0:T(1,128)S(1)} %get-tuple-element.21.total_ref, bf16[32,4,128,128]{3,2,1,0:T(8,128)(2,1)S(1)} %get-tuple-element.22.values_ref, ...), custom_call_target="tpu_custom_call" | custom-call | flops 2147483648 | bytes 16777216 | tf_op jit(solution)/shard_map/values_near/pallas_call | solution.py:228
  119.9 2.9 %project_far.1 = (bf16[128,2048]{1,0:T(8,128)(2,1)S(1)}, bf16[128,2048]{1,0:T(8,128)(2,1)S(1)}) custom-call(s32[5]{0:T(128)S(1)} %pad_add_fusion.place, bf16[128,1024]{1,0:T(8,128)(2,1)S(1)} %get-tuple-element.42.mine_ref, bf16[128,1024]{1,0:T(8,128)(2,1)S(1)} %collective-permute-done.13.theirs_ref, bf16[2048,4096]{1,0:T(8,128)(2,1)S(1)} %get-tuple-element.28.held_ref), custom_call_target="tpu_custom_call" | custom-call | flops 2147483648 | bytes 16777216 | tf_op jit(solution)/shard_map/project_far/pallas_call | solution.py:292
  125.6 11.5 %collective-permute-done.14.refs_0_ = bf16[128,2048]{1,0:T(8,128)(2,1)S(1)} collective-permute-done((bf16[128,2048]{1,0:T(8,128)(2,1)S(1)}, bf16[128,2048]{1,0:T(8,128)(2,1)S(1)}, u32[]{:S(2)}, u32[]{:S(2)}) %collective-permute-start.14) | collective-permute-done | bytes 524320 | tf_op jit(solution)/shard_map/ppermute | solution.py:336
  137.1 5.0 %project_near.1 = (bf16[128,4096]{1,0:T(8,128)(2,1)S(1)}, bf16[128,4096]{1,0:T(8,128)(2,1)S(1)}) custom-call(s32[5]{0:T(128)S(1)} %pad_add_fusion.place, bf16[256,1024]{1,0:T(8,128)(2,1)S(1)} %get-tuple-element.38.mine_ref, bf16[256,1024]{1,0:T(8,128)(2,1)S(1)} %collective-permute-done.12.theirs_ref, bf16[2048,4096]{1,0:T(8,128)(2,1)S(1)} %get-tuple-element.28.held_ref, ...), custom_call_target="tpu_custom_call" | custom-call | flops 4294967296 | bytes 16777216 | tf_op jit(solution)/shard_map/project_near/pallas_call | solution.py:292
  143.2 1.8 %collective-permute-start.17 = (bf16[128,4096]{1,0:T(8,128)(2,1)S(1)}, bf16[128,4096]{1,0:T(8,128)(2,1)S(1)}, u32[]{:S(2)}, u32[]{:S(2)}) collective-permute-start(bf16[128,4096]{1,0:T(8,128)(2,1)S(1)} %get-tuple-element.32), channel_id=1, source_target_pairs={{0,3},{1,0},{2,1},{3,2},{4,7},{5,4},{6,5},{7,6},{8,11},{9,8},{10,9... | collective-permute-start | bytes 3145736 | tf_op jit(solution)/shard_map/ppermute | solution.py:336
  145.0 8.0 %scores_own.1 = (bf16[8,2048,256]{2,1,0:T(8,128)(2,1)S(1)}, f32[8,1,256]{2,1,0:T(1,128)S(1)}) custom-call(s32[1024]{0:T(1024)S(1)} %reshape.76.lists, s32[64]{0:T(128)S(1)} %reshape.77.counts, s32[5]{0:T(128)S(1)} %pad_add_fusion.place, bf16[2,8,512,128]{3,2,1,0:T(8,128)(2,1)S(1)} %pad_maximum_fusion.q_ref, ...), custom_call_target="tpu_custom_call" | custom-call | flops 2147483648 | bytes 8388608 | tf_op jit(solution)/shard_map/scores_own/pallas_call | solution.py:110
  153.0 3.3 %copy-done.6 = bf16[8,2048,256]{2,1,0:T(8,128)(2,1)} copy-done((bf16[8,2048,256]{2,1,0:T(8,128)(2,1)}, bf16[8,2048,256]{2,1,0:T(8,128)(2,1)S(1)}, u32[]{:S(2)}) %copy-start.6) | copy-done | bytes 8388632
  156.3 3.4 %copy-done.7 = bf16[8,2048,256]{2,1,0:T(8,128)(2,1)S(1)} copy-done((bf16[8,2048,256]{2,1,0:T(8,128)(2,1)S(1)}, bf16[8,2048,256]{2,1,0:T(8,128)(2,1)}, u32[]{:S(2)}) %copy-start.7) | copy-done | bytes 8388632
  159.7 3.3 %values_own.1 = bf16[2,128,1024]{2,1,0:T(8,128)(2,1)S(1)} custom-call(s32[1024]{0:T(1024)S(1)} %reshape.75.lists, f32[8,1,256]{2,1,0:T(1,128)S(1)} %get-tuple-element.19.total_ref, bf16[32,4,128,128]{3,2,1,0:T(8,128)(2,1)S(1)} %get-tuple-element.22.values_ref, bf16[2,256,1024]{2,1,0:T(8,128)(2,1)S(1)} %get-tuple-element.26.after_ref, ...), custom_call_target="tpu_custom_call" | custom-call | flops 1073741824 | bytes 8388608 | tf_op jit(solution)/shard_map/values_own/pallas_call | solution.py:228
  163.0 1.9 %collective-permute-start.11 = (bf16[128,1024]{1,0:T(8,128)(2,1)S(1)}, bf16[128,1024]{1,0:T(8,128)(2,1)S(1)}, u32[]{:S(2)}, u32[]{:S(2)}) collective-permute-start(bf16[128,1024]{1,0:T(8,128)(2,1)S(1)} %get-tuple-element.39), channel_id=1, source_target_pairs={{0,4},{4,0},{8,12},{12,8},{16,20},{20,16},{24,28},{28,24},{32,36},... | collective-permute-start | bytes 786440 | tf_op jit(solution)/shard_map/ppermute | solution.py:332
  166.1 2.9 %project_own.1 = f32[128,4096]{1,0:T(8,128)S(1)} custom-call(s32[5]{0:T(128)S(1)} %pad_add_fusion.place, bf16[128,1024]{1,0:T(8,128)(2,1)S(1)} %get-tuple-element.40.mine_ref, bf16[128,1024]{1,0:T(8,128)(2,1)S(1)} %collective-permute-done.11.theirs_ref, bf16[2048,4096]{1,0:T(8,128)(2,1)S(1)} %get-tuple-element.28.held_ref), custom_call_target="tpu_custom_call" | custom-call | flops 2147483648 | bytes 16777216 | tf_op jit(solution)/shard_map/project_own/pallas_call | solution.py:292
  (75 shorter events, 18.8 us)
Async XLA Ops:
  6.5 13.1 %copy-start = (s32[16,128,16]{1,2,0:T(8,128)S(1)}, s32[16,128,16]{1,2,0:T(8,128)}, u32[]{:S(2)}) copy-start(s32[16,128,16]{1,2,0:T(8,128)} %param.10) | copy-start | bytes 393220
  6.5 83.1 %all-gather.3.cloned.1.call-start = ((), (), s32[]{:S(2)}) async-start(), calls=%async_computation | async-start | bytes 8650752 | tf_op jit(solution)/shard_map/all_gather | solution.py:361
  8.4 4.2 %copy-start.11 = (bf16[2,512,128]{2,1,0:T(8,128)(2,1)S(1)}, bf16[2,512,128]{2,1,0:T(8,128)(2,1)}, u32[]{:S(2)}) copy-start(bf16[2,512,128]{2,1,0:T(8,128)(2,1)} %param.8) | copy-start | bytes 786436
  8.4 4.4 %copy-start.13 = (s32[4]{0:T(128)S(1)}, s32[4]{0:T(128)}, u32[]{:S(2)}) copy-start(s32[4]{0:T(128)} %constant.170.clone) | copy-start | bytes 52
  11.2 30.9 %copy-start.12 = (s32[16,128]{1,0:T(8,128)S(1)}, s32[16,128]{1,0:T(8,128)}, u32[]{:S(2)}) copy-start(s32[16,128]{1,0:T(8,128)} %param.11) | copy-start | bytes 24580
  11.2 31.9 %collective-permute-start = (bf16[8,512,128]{2,1,0:T(8,128)(2,1)S(1)}, bf16[8,512,128]{2,1,0:T(8,128)(2,1)}, u32[]{:S(2)}, u32[]{:S(2)}) collective-permute-start(bf16[8,512,128]{2,1,0:T(8,128)(2,1)S(1)} %get-tuple-element.35), channel_id=1, source_target_pairs={{0,4},{4,0},{8,12},{12,8},{16,20},{20,16},{24,28},{28,24},{32,36},... | collective-permute-start | bytes 3145736 | tf_op jit(solution)/shard_map/ppermute | solution.py:332
  12.6 2.3 %collective-permute-start.1 = (bf16[4,128,128]{2,1,0:T(8,128)(2,1)S(1)}, bf16[4,128,128]{2,1,0:T(8,128)(2,1)S(1)}, u32[]{:S(2)}, u32[]{:S(2)}) collective-permute-start(bf16[4,128,128]{2,1,0:T(8,128)(2,1)S(1)} %get-tuple-element.44), channel_id=1, source_target_pairs={{0,4},{4,0},{8,12},{12,8},{16,20},{20,16},{24,28},{28,24},{32,36},... | collective-permute-start | bytes 393224 | tf_op jit(solution)/shard_map/ppermute | solution.py:332
  15.0 11.4 %collective-permute-start.3 = (bf16[8,128,128]{2,1,0:T(8,128)(2,1)S(1)}, bf16[8,128,128]{2,1,0:T(8,128)(2,1)S(1)}, u32[]{:S(2)}, u32[]{:S(2)}) collective-permute-start(bf16[8,128,128]{2,1,0:T(8,128)(2,1)S(1)} %pad_maximum_fusion.2.refs_0_), channel_id=1, source_target_pairs={{0,24},{4,100},{8,0},{12,108},{16,8},{20,116},{24,16},{28,124},{32... | collective-permute-start | bytes 786440 | tf_op jit(solution)/shard_map/ppermute | solution.py:328
  18.9 8.3 %collective-permute-start.4 = (bf16[8,128,128]{2,1,0:T(8,128)(2,1)S(1)}, bf16[8,128,128]{2,1,0:T(8,128)(2,1)S(1)}, u32[]{:S(2)}, u32[]{:S(2)}) collective-permute-start(bf16[8,128,128]{2,1,0:T(8,128)(2,1)S(1)} %pad_maximum_fusion.2.refs_0_), channel_id=1, source_target_pairs={{0,16},{4,68},{8,24},{12,76},{16,0},{20,84},{24,8},{28,92},{32,48}... | collective-permute-start | bytes 786440 | tf_op jit(solution)/shard_map/ppermute | solution.py:328
  18.9 11.7 %collective-permute-start.2 = (bf16[8,128,128]{2,1,0:T(8,128)(2,1)S(1)}, bf16[8,128,128]{2,1,0:T(8,128)(2,1)S(1)}, u32[]{:S(2)}, u32[]{:S(2)}) collective-permute-start(bf16[8,128,128]{2,1,0:T(8,128)(2,1)S(1)} %pad_maximum_fusion.2.refs_0_), channel_id=1, source_target_pairs={{0,8},{4,36},{8,16},{12,44},{16,24},{20,52},{24,0},{28,60},{32,40}... | collective-permute-start | bytes 786440 | tf_op jit(solution)/shard_map/ppermute | solution.py:328
  27.9 11.1 %collective-permute-start.8 = (bf16[16,128,128]{2,1,0:T(8,128)(2,1)}, bf16[16,128,128]{2,1,0:T(8,128)(2,1)}, u32[]{:S(2)}, u32[]{:S(2)}) collective-permute-start(bf16[16,128,128]{2,1,0:T(8,128)(2,1)} %constant_dynamic-update-slice_fusion), channel_id=1, source_target_pairs={{0,96},{4,28},{8,104},{12,4},{16,112},{20,12},{24,120},{28,20},{32... | collective-permute-start | bytes 1572872 | tf_op jit(solution)/shard_map/ppermute | solution.py:328
  31.5 10.6 %collective-permute-start.5 = (bf16[16,128,128]{2,1,0:T(8,128)(2,1)}, bf16[16,128,128]{2,1,0:T(8,128)(2,1)}, u32[]{:S(2)}, u32[]{:S(2)}) collective-permute-start(bf16[16,128,128]{2,1,0:T(8,128)(2,1)} %pad_maximum_fusion.1), channel_id=1, source_target_pairs={{0,32},{4,12},{8,40},{12,20},{16,48},{20,28},{24,56},{28,4},{32,64... | collective-permute-start | bytes 1572872 | tf_op jit(solution)/shard_map/ppermute | solution.py:328
  32.6 15.1 %collective-permute-start.6 = (bf16[16,128,128]{2,1,0:T(8,128)(2,1)}, bf16[16,128,128]{2,1,0:T(8,128)(2,1)}, u32[]{:S(2)}, u32[]{:S(2)}) collective-permute-start(bf16[16,128,128]{2,1,0:T(8,128)(2,1)} %constant_dynamic-update-slice_fusion), channel_id=1, source_target_pairs={{0,32},{4,12},{8,40},{12,20},{16,48},{20,28},{24,56},{28,4},{32,64... | collective-permute-start | bytes 1572872 | tf_op jit(solution)/shard_map/ppermute | solution.py:328
  33.9 13.8 %collective-permute-start.7 = (bf16[16,128,128]{2,1,0:T(8,128)(2,1)}, bf16[16,128,128]{2,1,0:T(8,128)(2,1)}, u32[]{:S(2)}, u32[]{:S(2)}) collective-permute-start(bf16[16,128,128]{2,1,0:T(8,128)(2,1)} %pad_maximum_fusion.1), channel_id=1, source_target_pairs={{0,96},{4,28},{8,104},{12,4},{16,112},{20,12},{24,120},{28,20},{32... | collective-permute-start | bytes 1572872 | tf_op jit(solution)/shard_map/ppermute | solution.py:328
  39.0 19.3 %collective-permute-start.10 = (bf16[16,128,128]{2,1,0:T(8,128)(2,1)}, bf16[16,128,128]{2,1,0:T(8,128)(2,1)}, u32[]{:S(2)}, u32[]{:S(2)}) collective-permute-start(bf16[16,128,128]{2,1,0:T(8,128)(2,1)} %collective-permute-done.8.refs_7_), channel_id=1, source_target_pairs={{0,96},{4,28},{8,104},{12,4},{16,112},{20,12},{24,120},{28,20},{32... | collective-permute-start | bytes 1572872 | tf_op jit(solution)/shard_map/ppermute | solution.py:328
  42.1 20.6 %collective-permute-start.9 = (bf16[16,128,128]{2,1,0:T(8,128)(2,1)}, bf16[16,128,128]{2,1,0:T(8,128)(2,1)}, u32[]{:S(2)}, u32[]{:S(2)}) collective-permute-start(bf16[16,128,128]{2,1,0:T(8,128)(2,1)} %collective-permute-done.5.refs_4_), channel_id=1, source_target_pairs={{0,32},{4,12},{8,40},{12,20},{16,48},{20,28},{24,56},{28,4},{32,64... | collective-permute-start | bytes 1572872 | tf_op jit(solution)/shard_map/ppermute | solution.py:328
  83.1 3.3 %copy-start.4 = (bf16[8,2048,256]{2,1,0:T(8,128)(2,1)}, bf16[8,2048,256]{2,1,0:T(8,128)(2,1)S(1)}, u32[]{:S(2)}) copy-start(bf16[8,2048,256]{2,1,0:T(8,128)(2,1)S(1)} %get-tuple-element.25.refs_1_) | copy-start | bytes 25165828
  86.4 3.2 %copy-start.9 = (bf16[8,2048,256]{2,1,0:T(8,128)(2,1)}, bf16[8,2048,256]{2,1,0:T(8,128)(2,1)S(1)}, u32[]{:S(2)}) copy-start(bf16[8,2048,256]{2,1,0:T(8,128)(2,1)S(1)} %get-tuple-element.20.weight_ref) | copy-start | bytes 25165828
  89.6 3.4 %copy-start.8 = (bf16[64,4,128,128]{3,2,1,0:T(8,128)(2,1)S(1)}, bf16[64,4,128,128]{3,2,1,0:T(8,128)(2,1)}, u32[]{:S(2)}) copy-start(bf16[64,4,128,128]{3,2,1,0:T(8,128)(2,1)} %all-gather.3.cloned.1.call-done) | copy-start | bytes 25165828
  93.0 3.4 %copy-start.10 = (bf16[8,2048,256]{2,1,0:T(8,128)(2,1)S(1)}, bf16[8,2048,256]{2,1,0:T(8,128)(2,1)}, u32[]{:S(2)}) copy-start(bf16[8,2048,256]{2,1,0:T(8,128)(2,1)} %copy-done.9) | copy-start | bytes 25165828
  100.2 19.7 %collective-permute-start.13 = (bf16[128,1024]{1,0:T(8,128)(2,1)S(1)}, bf16[128,1024]{1,0:T(8,128)(2,1)S(1)}, u32[]{:S(2)}, u32[]{:S(2)}) collective-permute-start(bf16[128,1024]{1,0:T(8,128)(2,1)S(1)} %get-tuple-element.41), channel_id=1, source_target_pairs={{0,4},{4,0},{8,12},{12,8},{16,20},{20,16},{24,28},{28,24},{32,36},... | collective-permute-start | bytes 786440 | tf_op jit(solution)/shard_map/ppermute | solution.py:332
  106.6 3.4 %copy-start.3 = (bf16[8,2048,256]{2,1,0:T(8,128)(2,1)S(1)}, bf16[8,2048,256]{2,1,0:T(8,128)(2,1)}, u32[]{:S(2)}) copy-start(bf16[8,2048,256]{2,1,0:T(8,128)(2,1)} %copy-done.2) | copy-start | bytes 25165828
  110.0 3.4 %copy-start.5 = (bf16[8,2048,256]{2,1,0:T(8,128)(2,1)S(1)}, bf16[8,2048,256]{2,1,0:T(8,128)(2,1)}, u32[]{:S(2)}) copy-start(bf16[8,2048,256]{2,1,0:T(8,128)(2,1)} %copy-done.4) | copy-start | bytes 25165828
  119.8 5.8 %collective-permute-start.12 = (bf16[256,1024]{1,0:T(8,128)(2,1)S(1)}, bf16[256,1024]{1,0:T(8,128)(2,1)S(1)}, u32[]{:S(2)}, u32[]{:S(2)}) collective-permute-start(bf16[256,1024]{1,0:T(8,128)(2,1)S(1)} %get-tuple-element.37), channel_id=1, source_target_pairs={{0,4},{4,0},{8,12},{12,8},{16,20},{20,16},{24,28},{28,24},{32,36},... | collective-permute-start | bytes 1572872 | tf_op jit(solution)/shard_map/ppermute | solution.py:332
  122.8 14.3 %collective-permute-start.14 = (bf16[128,2048]{1,0:T(8,128)(2,1)S(1)}, bf16[128,2048]{1,0:T(8,128)(2,1)S(1)}, u32[]{:S(2)}, u32[]{:S(2)}) collective-permute-start(bf16[128,2048]{1,0:T(8,128)(2,1)S(1)} %get-tuple-element.29), channel_id=1, source_target_pairs={{0,1},{1,2},{2,3},{3,0},{4,5},{5,6},{6,7},{7,4},{8,9},{9,10},{10,1... | collective-permute-start | bytes 1572872 | tf_op jit(solution)/shard_map/ppermute | solution.py:336
  124.2 12.9 %collective-permute-start.15 = (bf16[128,2048]{1,0:T(8,128)(2,1)S(1)}, bf16[128,2048]{1,0:T(8,128)(2,1)S(1)}, u32[]{:S(2)}, u32[]{:S(2)}) collective-permute-start(bf16[128,2048]{1,0:T(8,128)(2,1)S(1)} %get-tuple-element.30), channel_id=1, source_target_pairs={{0,3},{1,0},{2,1},{3,2},{4,7},{5,4},{6,5},{7,6},{8,11},{9,8},{10,9... | collective-permute-start | bytes 1572872 | tf_op jit(solution)/shard_map/ppermute | solution.py:336
  142.2 26.8 %collective-permute-start.16 = (bf16[128,4096]{1,0:T(8,128)(2,1)S(1)}, bf16[128,4096]{1,0:T(8,128)(2,1)S(1)}, u32[]{:S(2)}, u32[]{:S(2)}) collective-permute-start(bf16[128,4096]{1,0:T(8,128)(2,1)S(1)} %get-tuple-element.31), channel_id=1, source_target_pairs={{0,1},{1,2},{2,3},{3,0},{4,5},{5,6},{6,7},{7,4},{8,9},{9,10},{10,1... | collective-permute-start | bytes 3145736 | tf_op jit(solution)/shard_map/ppermute | solution.py:336
  143.2 25.8 %collective-permute-start.17 = (bf16[128,4096]{1,0:T(8,128)(2,1)S(1)}, bf16[128,4096]{1,0:T(8,128)(2,1)S(1)}, u32[]{:S(2)}, u32[]{:S(2)}) collective-permute-start(bf16[128,4096]{1,0:T(8,128)(2,1)S(1)} %get-tuple-element.32), channel_id=1, source_target_pairs={{0,3},{1,0},{2,1},{3,2},{4,7},{5,4},{6,5},{7,6},{8,11},{9,8},{10,9... | collective-permute-start | bytes 3145736 | tf_op jit(solution)/shard_map/ppermute | solution.py:336
  153.0 3.3 %copy-start.6 = (bf16[8,2048,256]{2,1,0:T(8,128)(2,1)}, bf16[8,2048,256]{2,1,0:T(8,128)(2,1)S(1)}, u32[]{:S(2)}) copy-start(bf16[8,2048,256]{2,1,0:T(8,128)(2,1)S(1)} %get-tuple-element.27.refs_0_) | copy-start | bytes 25165828
  156.3 3.4 %copy-start.7 = (bf16[8,2048,256]{2,1,0:T(8,128)(2,1)S(1)}, bf16[8,2048,256]{2,1,0:T(8,128)(2,1)}, u32[]{:S(2)}) copy-start(bf16[8,2048,256]{2,1,0:T(8,128)(2,1)} %copy-done.6) | copy-start | bytes 25165828
  163.0 3.1 %collective-permute-start.11 = (bf16[128,1024]{1,0:T(8,128)(2,1)S(1)}, bf16[128,1024]{1,0:T(8,128)(2,1)S(1)}, u32[]{:S(2)}, u32[]{:S(2)}) collective-permute-start(bf16[128,1024]{1,0:T(8,128)(2,1)S(1)} %get-tuple-element.39), channel_id=1, source_target_pairs={{0,4},{4,0},{8,12},{12,8},{16,20},{20,16},{24,28},{28,24},{32,36},... | collective-permute-start | bytes 786440 | tf_op jit(solution)/shard_map/ppermute | solution.py:332
  166.1 4.3 %copy-start.1 = (s32[16,128,16]{1,2,0:T(8,128)S(1)}, s32[16,128,16]{1,2,0:T(8,128)}, u32[]{:S(2)}) copy-start(s32[16,128,16]{1,2,0:T(8,128)} %param.10) | copy-start | bytes 393220
  (1 other events, 3.2 us)
Sparse Core Ops, SparseCore 0:
  9.6 64.4 all-gather.2

commit v3 on v1

v3 whole, which is shorter than its diff:
```python
import functools
import math

import jax
import jax.numpy as jnp
from jax import lax
from jax.experimental import pallas as pl
from jax.experimental.pallas import tpu as pltpu
from jax.sharding import PartitionSpec as P

BLK = 128
SLOTS = 16
PAIR = 2 * BLK
SPAN = SLOTS * BLK
RING = 4
CORES = 2
SEQ_DEVICES = RING * RING * CORES
CHUNK_COUPLES = 8
EXP2_SCALE = float(BLK ** -0.5 * math.log2(math.e))
LOW = -1e30
MIB = 2**20

SHORT = pl.CostEstimate(flops=1, bytes_accessed=1, transcendentals=0)

VMEM = pl.BlockSpec(memory_space=pltpu.VMEM)
HBM = pl.BlockSpec(memory_space=pltpu.HBM)


def stay(array):
    return pltpu.with_memory_space_constraint(array, pltpu.HBM)


def cat(parts, axis):
    return jnp.concatenate(parts, axis)


def score_couple(couple, lists, counts, place, q_ref, table, score_ref, top_ref):
    key_row = lax.broadcasted_iota(jnp.int32, (BLK, PAIR), 0)
    query_row = lax.broadcasted_iota(jnp.int32, (BLK, PAIR), 1) % BLK
    zero = jnp.zeros((BLK, BLK), jnp.bfloat16)
    chunk = couple // CHUNK_COUPLES
    side = (couple // 4) % 2
    head = 2 * (couple % 4)
    rows = pl.ds(pl.multiple_of(place[1 + chunk] * BLK, BLK), BLK)
    qa = q_ref[side, head, rows, :].T
    qb = q_ref[side, head + 1, rows, :].T
    queries = cat([cat([qa, zero], 1), cat([zero, qb], 1)], 0)
    a = 2 * couple * SLOTS
    keys = cat(
        [cat([table[lists[a + n]], table[lists[a + SLOTS + n]]], 1) for n in range(SLOTS)], 0
    )
    scores = jnp.dot(keys, queries, preferred_element_type=jnp.float32)
    count = live_counts(couple, counts)
    top = None
    for n in range(SLOTS):
        tile = scores[n * BLK : (n + 1) * BLK]
        if n == 0:
            tile = jnp.where(key_row <= query_row, tile, LOW)
            top = tile.reshape(16, 8, PAIR).max(0)
        else:
            best = tile.reshape(16, 8, PAIR).max(0)
            top = jnp.maximum(top, jnp.where(n < count, best, LOW))
        score_ref[n * BLK : (n + 1) * BLK, :] = tile
    top_ref[...] = jnp.max(top, axis=0, keepdims=True)


def live_counts(couple, counts):
    lane = lax.broadcasted_iota(jnp.int32, (1, PAIR), 1)
    return jnp.where(lane < BLK, counts[2 * couple], counts[2 * couple + 1])


def weigh_couple(couple, counts, score_ref, top_ref):
    count = live_counts(couple, counts)
    top = top_ref[...]
    total = jnp.zeros((8, PAIR), jnp.float32)
    tiles = []
    for n in range(SLOTS):
        shift = top if n == 0 else jnp.where(n < count, top, -LOW)
        weights = jnp.exp2((score_ref[n * BLK : (n + 1) * BLK, :] - shift) * EXP2_SCALE)
        total += weights.reshape(16, 8, PAIR).sum(0)
        tiles.append(weights.astype(jnp.bfloat16))
    return tiles, jnp.sum(total, axis=0, keepdims=True)


def combine_couple(couple, weights, total, lists, values, out_ref):
    side = (couple // 4) % 2
    head = 2 * (couple % 4)
    for half in range(2):
        pair = 2 * couple + half
        tiles = cat([values[lists[pair * SLOTS + n]] for n in range(SLOTS)], 1)
        lanes = slice(half * BLK, (half + 1) * BLK)
        summed = jnp.dot(tiles, weights[:, lanes], preferred_element_type=jnp.float32)
        attended = (summed / total[:, lanes]).T.astype(jnp.bfloat16)
        cols = pl.ds(pl.multiple_of((head + half) * BLK, BLK), BLK)
        out_ref[side, :, cols] = attended


def pipelined(first, score, weigh, buffers):
    score_a, top_a, score_b, top_b = buffers
    last = first + CHUNK_COUPLES - 1
    score(first, score_a, top_a)

    def step(index, carry):
        couple = first + 2 * index
        score(couple + 1, score_b, top_b)
        weigh(couple, score_a, top_a)
        score(jnp.minimum(couple + 2, last), score_a, top_a)
        weigh(couple + 1, score_b, top_b)
        return carry

    lax.fori_loop(0, CHUNK_COUPLES // 2, step, 0)


BUFFERS = [pltpu.VMEM((SPAN, PAIR), jnp.float32), pltpu.VMEM((1, PAIR), jnp.float32)] * 2


def hold_kernel(source_ref, after_ref, out_ref, sem):
    copy = pltpu.make_async_copy(source_ref, out_ref, sem)
    copy.start()
    copy.wait()


def hold_call(source, after):
    return pl.pallas_call(
        hold_kernel,
        name="hold_weight",
        in_specs=[HBM, HBM],
        out_specs=VMEM,
        out_shape=pltpu.VMEM(source.shape, source.dtype),
        scratch_shapes=[pltpu.SemaphoreType.DMA],
        compiler_params=pltpu.CompilerParams(vmem_limit_bytes=4 * MIB),
    )(stay(source), after)


def prepare_kernel(place, key_ref, value_ref, mine_ref, theirs_ref):
    core = place[0]
    for out_ref, head in ((mine_ref, core), (theirs_ref, 1 - core)):
        for block in range(out_ref.shape[1]):
            rows = slice(block * BLK, (block + 1) * BLK)
            out_ref[0, block] = key_ref[head, rows, :]
            out_ref[1, block] = value_ref[head, rows, :].T


def prepare_call(place, keys, values):
    blocks = keys.shape[1] // BLK
    shape = jax.ShapeDtypeStruct((2, blocks, BLK, BLK), jnp.bfloat16)
    return pl.pallas_call(
        prepare_kernel,
        name="prepare",
        grid_spec=pltpu.PrefetchScalarGridSpec(
            num_scalar_prefetch=1, grid=(1,), in_specs=[VMEM] * 2, out_specs=[VMEM] * 2
        ),
        out_shape=[shape, shape],
        compiler_params=pltpu.CompilerParams(vmem_limit_bytes=6 * MIB),
    )(place, keys, values)


def bring(pieces, tables, sems, places):
    copies = []
    for index, (piece, (table, at)) in enumerate(zip(pieces, places)):
        copies.append(
            pltpu.make_async_copy(
                piece, tables[table].at[pl.ds(at, piece.shape[0])], sems.at[index]
            )
        )
    for copy in copies:
        copy.start()
    for copy in copies:
        copy.wait()


def tables_kernel(places, *refs):
    pieces, tables, sems = refs[: len(places)], refs[len(places) : -1], refs[-1]
    bring(pieces, tables, sems, places)


def tables_call(places, pieces):
    return pl.pallas_call(
        functools.partial(tables_kernel, places),
        name="tables",
        in_specs=[HBM] * len(pieces),
        out_specs=[VMEM] * 2,
        out_shape=[pltpu.VMEM((BLK, BLK, BLK), jnp.bfloat16)] * 2,
        scratch_shapes=[pltpu.SemaphoreType.DMA((len(pieces),))],
        compiler_params=pltpu.CompilerParams(vmem_limit_bytes=4 * MIB),
        cost_estimate=SHORT,
    )(*map(stay, pieces))


def attend_kernel(first, places, lists, counts, place, q_ref, after_ref, *refs):
    if places:
        pieces, refs = refs[: len(places)], refs[len(places) + 2 :]
        out_ref, keys, values, *buffers, sems = refs
        bring(pieces, (keys, values), sems, places)
    else:
        keys, values, out_ref, *buffers = refs

    def score(couple, score_ref, top_ref):
        score_couple(couple, lists, counts, place, q_ref, keys, score_ref, top_ref)

    def weigh(couple, score_ref, top_ref):
        tiles, total = weigh_couple(couple, counts, score_ref, top_ref)
        combine_couple(couple, cat(tiles, 0), total, lists, values, out_ref)

    pipelined(first, score, weigh, buffers)


def attend_call(name, chunk, lists, counts, place, queries, after, tables, pieces=(), places=()):
    out_shape = [jax.ShapeDtypeStruct((2, BLK, 8 * BLK), jnp.bfloat16)]
    scratch = list(BUFFERS)
    aliases = {}
    if pieces:
        out_shape += [pltpu.VMEM(table.shape, table.dtype) for table in tables]
        scratch += [pltpu.SemaphoreType.DMA((len(pieces),))]
        aliases = {5 + len(pieces): 1, 6 + len(pieces): 2}
    return pl.pallas_call(
        functools.partial(attend_kernel, chunk * CHUNK_COUPLES, places),
        name=name,
        grid_spec=pltpu.PrefetchScalarGridSpec(
            num_scalar_prefetch=3,
            grid=(1,),
            in_specs=[VMEM, VMEM if pieces else HBM] + [HBM] * len(pieces) + [VMEM] * len(tables),
            out_specs=[VMEM] * len(out_shape),
            scratch_shapes=scratch,
        ),
        out_shape=out_shape,
        input_output_aliases=aliases,
        compiler_params=pltpu.CompilerParams(vmem_limit_bytes=10 * MIB),
        cost_estimate=SHORT,
    )(lists, counts, place, queries, after, *map(stay, pieces), *tables)


def queries_kernel(place, source_ref, after_ref, mine_ref, theirs_ref, sems):
    heads = mine_ref.shape[0]
    core = place[0]
    copies = [
        pltpu.make_async_copy(
            source_ref.at[pl.ds(owner * heads, heads)], out_ref, sems.at[index]
        )
        for index, (owner, out_ref) in enumerate(((core, mine_ref), (1 - core, theirs_ref)))
    ]
    for copy in copies:
        copy.start()
    for copy in copies:
        copy.wait()


def queries_call(place, queries, heads, after):
    shape = jax.ShapeDtypeStruct((heads,) + queries.shape[1:], queries.dtype)
    return pl.pallas_call(
        queries_kernel,
        name="queries",
        grid_spec=pltpu.PrefetchScalarGridSpec(
            num_scalar_prefetch=1,
            grid=(1,),
            in_specs=[HBM, HBM],
            out_specs=[VMEM, VMEM],
            scratch_shapes=[pltpu.SemaphoreType.DMA((2,))],
        ),
        out_shape=[shape, shape],
        compiler_params=pltpu.CompilerParams(vmem_limit_bytes=8 * MIB),
        cost_estimate=SHORT,
    )(place, stay(queries), after)


def project_kernel(kind, place, mine_ref, theirs_ref, held_ref, after_ref, *refs):
    width = held_ref.shape[1]
    tile = 1024
    core = place[0]
    mine = mine_ref[...]
    theirs = theirs_ref[...]
    both = cat([jnp.where(core == 0, mine, theirs), jnp.where(core == 0, theirs, mine)], 1)
    for at in range(0, width, tile):
        cols = slice(at, at + tile)
        low = at < width // 2
        near = slice(at % (width // 2), at % (width // 2) + tile)
        total = jnp.dot(both, held_ref[:, cols], preferred_element_type=jnp.float32)
        if kind == "far":
            refs[0 if low else 1][:, near] = total.astype(jnp.bfloat16)
        elif kind == "own":
            refs[0][:, cols] = total
        else:
            if low == (kind == "up"):
                total = total + refs[0][:, near].astype(jnp.float32)
            refs[1][:, cols] = total.astype(jnp.bfloat16)


def project_call(kind, place, mine, theirs, held, after, *arrived):
    width = held.shape[1]
    shapes = {
        "far": [((BLK, width // 2), jnp.bfloat16)] * 2,
        "up": [((BLK, width), jnp.bfloat16)],
        "down": [((BLK, width), jnp.bfloat16)],
        "own": [((BLK, width), jnp.float32)],
    }[kind]
    return pl.pallas_call(
        functools.partial(project_kernel, kind),
        name="project_" + kind,
        grid_spec=pltpu.PrefetchScalarGridSpec(
            num_scalar_prefetch=1,
            grid=(1,),
            in_specs=[VMEM] * 3 + [HBM] + [VMEM] * len(arrived),
            out_specs=[VMEM] * len(shapes),
        ),
        out_shape=[jax.ShapeDtypeStruct(*shape) for shape in shapes],
        compiler_params=pltpu.CompilerParams(vmem_limit_bytes=8 * MIB),
        cost_estimate=SHORT,
    )(place, mine, theirs, held, after, *arrived)


def chip_perm(phase, step):
    pairs = []
    for z in range(RING):
        for y in range(RING):
            for core in range(CORES):
                if (core == 0) == (phase == 0):
                    to_z, to_y = z, (y + step) % RING
                else:
                    to_z, to_y = (z + step) % RING, y
                pairs.append(((z * RING + y) * CORES + core, (to_z * RING + to_y) * CORES + core))
    return pairs


SWAP = [(i, i ^ 1) for i in range(SEQ_DEVICES)]


def along(array, phase, step):
    return lax.ppermute(array, "seq", chip_perm(phase, step))


def swap(array):
    return lax.ppermute(array, "seq", SWAP)


def turn(array, step):
    return lax.ppermute(array, "grp", [(i, (i + step) % RING) for i in range(RING)])


def gather_tiles(own):
    parts = [own, along(own, 0, 1), along(own, 0, -1), along(own, 0, 2)]
    keys = cat([part[0] for part in parts], 0)
    values = cat([part[1] for part in parts], 0)
    keys_left, values_right = along(keys, 1, 1), along(values, 1, -1)
    values_left, keys_right = along(values, 1, 1), along(keys, 1, -1)
    keys_far, values_far = along(keys_left, 1, 1), along(values_right, 1, -1)
    size = keys.shape[0]
    early = [keys, keys_left, keys_right, values, values_left, values_right]
    early_places = ((0, 0), (0, size), (0, 2 * size), (1, 0), (1, size), (1, 2 * size))
    late = [keys_far, values_far]
    late_places = ((0, 3 * size), (1, 3 * size))
    return parts[1], early, early_places, late, late_places


def body(query_states, key_states, value_states, tile_keys, tile_count, out_weight):
    head_group, row_count, width = query_states.shape
    kv_group = key_states.shape[0]
    blocks = row_count // BLK
    heads = head_group // kv_group
    seq_place = lax.axis_index("seq")
    grp_place = lax.axis_index("grp")
    core = seq_place % CORES
    chip = seq_place // CORES
    chip_z, chip_y = chip // RING, chip % RING

    chunks = (grp_place + jnp.array([2, 1, 3, 0], jnp.int32)) % RING
    place = jnp.concatenate([core[None], chunks]).astype(jnp.int32)
    mine, theirs = prepare_call(place, key_states, value_states)
    first, early, early_places, late, late_places = gather_tiles(cat([mine, swap(theirs)], 1))

    queries_mine, queries_theirs = queries_call(place, query_states, heads, first)
    queries = jnp.stack([swap(queries_theirs), queries_mine])

    sides = jnp.stack([1 - core, core])
    order = (chip * 2 * blocks + sides[None, :] * blocks + chunks[:, None]).reshape(-1)
    my_lists = lax.dynamic_slice_in_dim(tile_keys, core * heads, heads, 0)
    my_counts = lax.dynamic_slice_in_dim(tile_count, core * heads, heads, 0)
    lists = jnp.swapaxes(jnp.take(my_lists, order, axis=1), 0, 1)
    counts = jnp.swapaxes(jnp.take(my_counts, order, axis=1), 0, 1).reshape(-1)

    span = 2 * blocks
    from_chip = lists // span
    inside = lists % span
    step_z = (from_chip // RING - chip_z) % RING
    step_y = (from_chip % RING - chip_y) % RING

    def arrival(step):
        return jnp.where(step == 1, 2, jnp.where(step == 2, 3, jnp.where(step == 3, 1, 0)))

    inner = arrival(jnp.where(core == 0, step_y, step_z))
    outer = arrival(jnp.where(core == 0, step_z, step_y))
    lists = (
        (outer * RING + inner) * span
        + (inside // blocks + core) % CORES * blocks
        + inside % blocks
    ).reshape(-1)

    held = hold_call(out_weight, first)

    tables = tables_call(early_places, early)
    far_att, *tables = attend_call(
        "attend_far", 0, lists, counts, place, queries, held, tables, late, late_places
    )

    def attend(name, chunk, after):
        return attend_call(name, chunk, lists, counts, place, queries, after, tables)

    low, high = project_call("far", place, far_att[1], swap(far_att[0]), held, far_att)
    low_in, high_in = turn(low, 1), turn(high, -1)
    (up_att,) = attend("attend_up", 1, low)
    (down_att,) = attend("attend_down", 2, up_att)
    (up,) = project_call("up", place, up_att[1], swap(up_att[0]), held, down_att, low_in)
    from_left = turn(up, 1)
    (down,) = project_call("down", place, down_att[1], swap(down_att[0]), held, up, high_in)
    from_right = turn(down, -1)
    (own_att,) = attend("attend_own", 3, down)
    (own,) = project_call("own", place, own_att[1], swap(own_att[0]), held, own_att)
    total = own + from_left.astype(jnp.float32) + from_right.astype(jnp.float32)
    return total.astype(jnp.bfloat16)


def solution(mesh):
    placed = (
        P("grp", "seq", None),
        P("grp", "seq", None),
        P("grp", "seq", None),
        P("grp", None, None),
        P("grp", None),
        P("grp", None),
    )
    return jax.shard_map(
        body, mesh=mesh, in_specs=placed, out_specs=P(("seq", "grp"), None), check_vma=False
    )
```

time: 188 us -> 135 us (0.72)
  waiting for transfers between devices: 120 us -> 42.3 us
  starting transfers between devices: 0.04 us -> 25.4 us
  Pallas kernels: 34.7 us -> 56.6 us
  matrix products: 14.4 us -> 0 us
  between operations: 13.4 us -> 0.27 us
  other arithmetic: 1.89 us -> 6.24 us
    all_gather x1 -> x0, waiting for transfers between devices: 73.8 us -> none  [body(): gathered = lax.all_gather(local, 'seq', axis=0, tiled=False)]
    reduce_scatter x1 -> x0, waiting for transfers between devices: 46 us -> none  [body(): lax.psum_scatter(partial.astype(jnp.bfloat16), 'grp', scatter_dimension=0...]
    ppermute x0 -> x19, waiting for transfers between devices: none -> 42.3 us  [the longest x9 25.6 us: along(): return lax.ppermute(array, 'seq', chip_perm(phase, step))]
    ppermute x0 -> x19, starting transfers between devices: none -> 25.4 us  [the longest x9 12.1 us: along(): return lax.ppermute(array, 'seq', chip_perm(phase, step))]
    pallas_call x1 -> x12, Pallas kernels: 34.7 us -> 56.6 us  [the longest x4 33.2 us: attend_call(): pl.pallas_call(functools.partial(attend_kernel, chunk * CHUNK_COUPLES, pl...]
    dot_general x1 -> x0, matrix products: 14.4 us -> none  [body(): partial = jnp.dot(attended, out_weight, preferred_element_type=jnp.float32)]
    reshape x3 -> x2, local copies, waits for them, and re-layouts: 2.51 us -> 0.16 us  [the longest x1 0.08 us: body(): counts = jnp.swapaxes(jnp.take(my_counts, order, axis=1), 0, 1).reshape(-1)]
    concatenate x0 -> x3, other arithmetic: none -> 2.3 us  [the longest x2 2.22 us: cat(): return jnp.concatenate(parts, axis)]
  transfers between devices with their start and end apart: 2 -> 19, of which waited for: 2 -> 13; matrix products, arithmetic and copies ran while one was open for 1% -> 4% of each run, Pallas kernels for 0% -> 30%
where the time goes in v3:
time: 135 us
  Pallas kernels  56.6 us (42%)
  waiting for transfers between devices  42.3 us (31%)
  starting transfers between devices  25.4 us (19%)
  other arithmetic  6.24 us (5%)
  local copies, waits for them, and re-layouts  4.04 us (3%)
    pallas_call x4, Pallas kernels, attend_call(): pl.pallas_call(functools.partial(attend_kernel, chunk * CHUNK_COUPLES, pl...  33.2 us
    ppermute x9, waiting for transfers between devices, along(): return lax.ppermute(array, 'seq', chip_perm(phase, step))  25.6 us
    ppermute x4, waiting for transfers between devices, turn(): lax.ppermute(array, 'grp', [(i, (i + step) % RING) for i in range(RING)])  12.2 us
    ppermute x9, starting transfers between devices, along(): return lax.ppermute(array, 'seq', chip_perm(phase, step))  12.1 us
    pallas_call x4, Pallas kernels, project_call(): pl.pallas_call(functools.partial(project_kernel, kind), name='project_' +...  12 us
    ppermute x6, starting transfers between devices, swap(): return lax.ppermute(array, 'seq', SWAP)  7.73 us
    pallas_call x1, Pallas kernels, hold_call(): pl.pallas_call(hold_kernel, name='hold_weight', in_specs=[HBM, HBM], out_...  5.78 us
    ppermute x4, starting transfers between devices, turn(): lax.ppermute(array, 'grp', [(i, (i + step) % RING) for i in range(RING)])  5.58 us
  transfers between devices with their start and end apart: 19, of which 13 were waited for; matrix products, arithmetic and copies ran while one was open for 4% of the time, Pallas kernels for 30%

profile of v3, /device:TPU:1, one launch (start us, length us, event | category | flops | bytes accessed | tf_op | source)
XLA Modules:
  0.0 134.9 jit_solution(4544440958908949199)
XLA Ops:
  3.4 1.5 %collective-permute-start = (bf16[2,4,128,128]{3,2,1,0:T(8,128)(2,1)S(1)}, bf16[2,4,128,128]{3,2,1,0:T(8,128)(2,1)S(1)}, u32[]{:S(2)}, u32[]{:S(2)}) collective-permute-start(bf16[2,4,128,128]{3,2,1,0:T(8,128)(2,1)S(1)} %get-tuple-element.17), channel_id=1, source_target_pairs={{0,4},{4,0},{8,12},{12,8},{16,20},{20,16},{24,28},{28,24},{32,36},... | collective-permute-start | bytes 786440 | tf_op jit(solution)/shard_map/ppermute | solution.py:332
  4.9 1.1 collective-permute-done
  6.1 3.8 %collective-permute-start.4 = (bf16[2,8,128,128]{3,2,1,0:T(8,128)(2,1)S(1)}, bf16[2,8,128,128]{3,2,1,0:T(8,128)(2,1)S(1)}, u32[]{:S(2)}, u32[]{:S(2)}) collective-permute-start(bf16[2,8,128,128]{3,2,1,0:T(8,128)(2,1)S(1)} %constant_dynamic-update-slice_fusion), channel_id=1, source_target_pairs={{0,16},{4,68},{8,24},{12,76},{16,0},{20,84},{24,8},{28,92},{32,48}... | collective-permute-start | bytes 1572872 | tf_op jit(solution)/shard_map/ppermute | solution.py:328
  11.3 5.4 %collective-permute-done.4 = bf16[2,8,128,128]{3,2,1,0:T(8,128)(2,1)S(1)} collective-permute-done((bf16[2,8,128,128]{3,2,1,0:T(8,128)(2,1)S(1)}, bf16[2,8,128,128]{3,2,1,0:T(8,128)(2,1)S(1)}, u32[]{:S(2)}, u32[]{:S(2)}) %collective-permute-start.4) | collective-permute-done | bytes 524320 | tf_op jit(solution)/shard_map/ppermute | solution.py:328
  16.8 6.1 %collective-permute-done.3 = bf16[2,8,128,128]{3,2,1,0:T(8,128)(2,1)S(1)} collective-permute-done((bf16[2,8,128,128]{3,2,1,0:T(8,128)(2,1)S(1)}, bf16[2,8,128,128]{3,2,1,0:T(8,128)(2,1)S(1)}, u32[]{:S(2)}, u32[]{:S(2)}) %collective-permute-start.3) | collective-permute-done | bytes 524320 | tf_op jit(solution)/shard_map/ppermute | solution.py:328
  24.1 1.2 collective-permute-start.5
  26.4 1.5 %collective-permute-start.7 = (bf16[32,128,128]{2,1,0:T(8,128)(2,1)}, bf16[32,128,128]{2,1,0:T(8,128)(2,1)}, u32[]{:S(2)}, u32[]{:S(2)}) collective-permute-start(bf16[32,128,128]{2,1,0:T(8,128)(2,1)} %pad_maximum_fusion.2.refs_3_), channel_id=1, source_target_pairs={{0,96},{4,28},{8,104},{12,4},{16,112},{20,12},{24,120},{28,20},{32... | collective-permute-start | bytes 3145736 | tf_op jit(solution)/shard_map/ppermute | solution.py:328
  28.3 1.5 %collective-permute-start.9 = (bf16[32,128,128]{2,1,0:T(8,128)(2,1)}, bf16[32,128,128]{2,1,0:T(8,128)(2,1)}, u32[]{:S(2)}, u32[]{:S(2)}) collective-permute-start(bf16[32,128,128]{2,1,0:T(8,128)(2,1)} %pad_maximum_fusion.1.refs_0_), channel_id=1, source_target_pairs={{0,96},{4,28},{8,104},{12,4},{16,112},{20,12},{24,120},{28,20},{32... | collective-permute-start | bytes 3145736 | tf_op jit(solution)/shard_map/ppermute | solution.py:328
  29.9 2.1 %queries.1 = (bf16[8,512,128]{2,1,0:T(8,128)(2,1)S(1)}, bf16[8,512,128]{2,1,0:T(8,128)(2,1)S(1)}) custom-call(s32[5]{0:T(128)S(1)} %pad_add_fusion.place, bf16[16,512,128]{2,1,0:T(8,128)(2,1)} %source_ref.2, bf16[2,8,128,128]{3,2,1,0:T(8,128)(2,1)S(1)} %collective-permute-done.1.after_ref), custom_call_target="tpu_custom_call" | custom-call | flops 1 | bytes 1 | tf_op jit(solution)/shard_map/queries/pallas_call | solution.py:250
  32.0 2.4 %collective-permute-start.2 = (bf16[8,512,128]{2,1,0:T(8,128)(2,1)S(1)}, bf16[8,512,128]{2,1,0:T(8,128)(2,1)}, u32[]{:S(2)}, u32[]{:S(2)}) collective-permute-start(bf16[8,512,128]{2,1,0:T(8,128)(2,1)S(1)} %get-tuple-element.18), channel_id=1, source_target_pairs={{0,4},{4,0},{8,12},{12,8},{16,20},{20,16},{24,28},{28,24},{32,36},... | collective-permute-start | bytes 3145736 | tf_op jit(solution)/shard_map/ppermute | solution.py:332
  34.4 5.2 %collective-permute-done.5.refs_1_ = bf16[32,128,128]{2,1,0:T(8,128)(2,1)} collective-permute-done((bf16[32,128,128]{2,1,0:T(8,128)(2,1)}, bf16[32,128,128]{2,1,0:T(8,128)(2,1)}, u32[]{:S(2)}, u32[]{:S(2)}) %collective-permute-start.5) | collective-permute-done | bytes 1048608 | tf_op jit(solution)/shard_map/ppermute | solution.py:328
  40.7 2.7 %collective-permute-start.8 = (bf16[32,128,128]{2,1,0:T(8,128)(2,1)}, bf16[32,128,128]{2,1,0:T(8,128)(2,1)}, u32[]{:S(2)}, u32[]{:S(2)}) collective-permute-start(bf16[32,128,128]{2,1,0:T(8,128)(2,1)} %collective-permute-done.7.refs_5_), channel_id=1, source_target_pairs={{0,96},{4,28},{8,104},{12,4},{16,112},{20,12},{24,120},{28,20},{32... | collective-permute-start | bytes 3145736 | tf_op jit(solution)/shard_map/ppermute | solution.py:328
  45.2 5.8 %hold_weight.1.after_ref.held_ref = bf16[2048,4096]{1,0:T(8,128)(2,1)S(1)} custom-call(bf16[2048,4096]{1,0:T(8,128)(2,1)} %source_ref.3, bf16[2,8,128,128]{3,2,1,0:T(8,128)(2,1)S(1)} %collective-permute-done.1.after_ref), custom_call_target="tpu_custom_call" | custom-call | tf_op jit(solution)/shard_map/hold_weight/pallas_call | solution.py:124
  51.9 2.9 %tables.1 = (bf16[128,128,128]{2,1,0:T(8,128)(2,1)S(1)}, bf16[128,128,128]{2,1,0:T(8,128)(2,1)S(1)}) custom-call(bf16[32,128,128]{2,1,0:T(8,128)(2,1)} %pad_maximum_fusion.1.refs_0_, bf16[32,128,128]{2,1,0:T(8,128)(2,1)} %collective-permute-done.5.refs_1_, bf16[32,128,128]{2,1,0:T(8,128)(2,1)} %collective-permute-done.9.refs_2_, ...), custom_call_target="tpu_custom_call" | custom-call | flops 1 | bytes 1 | tf_op jit(solution)/shard_map/tables/pallas_call | solution.py:178
  54.8 1.4 %pad_maximum_fusion.q_ref = bf16[2,8,512,128]{3,2,1,0:T(8,128)(2,1)S(1)} fusion(bf16[1,8,512,128]{3,2,1,0:T(8,128)(2,1)S(1)} %bitcast.38, bf16[1,8,512,128]{3,2,1,0:T(8,128)(2,1)} %bitcast.3), kind=kLoop, calls=%fused_computation.2 | loop fusion | flops 1048576 | bytes 4194304 | tf_op jit(solution)/shard_map/stack | solution.py:371
  56.2 5.8 %collective-permute-done.6.refs_0_ = bf16[32,128,128]{2,1,0:T(8,128)(2,1)} collective-permute-done((bf16[32,128,128]{2,1,0:T(8,128)(2,1)}, bf16[32,128,128]{2,1,0:T(8,128)(2,1)}, u32[]{:S(2)}, u32[]{:S(2)}) %collective-permute-start.6) | collective-permute-done | bytes 1048608 | tf_op jit(solution)/shard_map/ppermute | solution.py:328
  63.1 9.5 %attend_far.1 = (bf16[2,128,1024]{2,1,0:T(8,128)(2,1)S(1)}, bf16[128,128,128]{2,1,0:T(8,128)(2,1)S(1)}, bf16[128,128,128]{2,1,0:T(8,128)(2,1)S(1)}) custom-call(s32[1024]{0:T(1024)S(1)} %reshape.66.lists, s32[64]{0:T(128)S(1)} %reshape.67.counts, s32[5]{0:T(128)S(1)} %pad_add_fusion.place, ...), custom_call_target="tpu_custom_call", output_to_operand_aliasing={{1}: (7, {}), {2}: (8, {})} | custom-call | flops 1 | bytes 1 | tf_op jit(solution)/shard_map/attend_far/pallas_call | solution.py:216
  72.7 2.0 %collective-permute-start.11 = (bf16[128,1024]{1,0:T(8,128)(2,1)S(1)}, bf16[128,1024]{1,0:T(8,128)(2,1)S(1)}, u32[]{:S(2)}, u32[]{:S(2)}) collective-permute-start(bf16[128,1024]{1,0:T(8,128)(2,1)S(1)} %get-tuple-element.33), channel_id=1, source_target_pairs={{0,4},{4,0},{8,12},{12,8},{16,20},{20,16},{24,28},{28,24},{32,36},... | collective-permute-start | bytes 786440 | tf_op jit(solution)/shard_map/ppermute | solution.py:332
  74.8 1.2 collective-permute-done.11.theirs_ref
  75.9 3.0 %project_far.1 = (bf16[128,2048]{1,0:T(8,128)(2,1)S(1)}, bf16[128,2048]{1,0:T(8,128)(2,1)S(1)}) custom-call(s32[5]{0:T(128)S(1)} %pad_add_fusion.place, bf16[128,1024]{1,0:T(8,128)(2,1)S(1)} %get-tuple-element.34.mine_ref, bf16[128,1024]{1,0:T(8,128)(2,1)S(1)} %collective-permute-done.11.theirs_ref, bf16[2048,4096]{1,0:T(8,128)(2,1)S(1)} %hold_weight.1.after_ref.held_ref, ...), custom_call_target="tpu_custom_call" | custom-call | flops 1 | bytes 1 | tf_op jit(solution)/shard_map/project_far/pallas_call | solution.py:296
  79.0 2.6 %collective-permute-start.15 = (bf16[128,2048]{1,0:T(8,128)(2,1)S(1)}, bf16[128,2048]{1,0:T(8,128)(2,1)S(1)}, u32[]{:S(2)}, u32[]{:S(2)}) collective-permute-start(bf16[128,2048]{1,0:T(8,128)(2,1)S(1)} %get-tuple-element.26), channel_id=1, source_target_pairs={{0,3},{1,0},{2,1},{3,2},{4,7},{5,4},{6,5},{7,6},{8,11},{9,8},{10,9... | collective-permute-start | bytes 1572872 | tf_op jit(solution)/shard_map/ppermute | solution.py:336
  81.5 7.9 %attend_up.1.after_ref = bf16[2,128,1024]{2,1,0:T(8,128)(2,1)S(1)} custom-call(s32[1024]{0:T(1024)S(1)} %reshape.66.lists, s32[64]{0:T(128)S(1)} %reshape.67.counts, s32[5]{0:T(128)S(1)} %pad_add_fusion.place, bf16[2,8,512,128]{3,2,1,0:T(8,128)(2,1)S(1)} %pad_maximum_fusion.q_ref, bf16[128,2048]{1,0:T(8,128)(2,1)S(1)} %get-tuple-element.23.after_ref, ...), custom_call_target="tpu_custom_call" | custom-call | flops 1 | bytes 1 | tf_op jit(solution)/shard_map/attend_up/pallas_call | solution.py:216
  89.5 7.9 %attend_down.1.after_ref = bf16[2,128,1024]{2,1,0:T(8,128)(2,1)S(1)} custom-call(s32[1024]{0:T(1024)S(1)} %reshape.66.lists, s32[64]{0:T(128)S(1)} %reshape.67.counts, s32[5]{0:T(128)S(1)} %pad_add_fusion.place, bf16[2,8,512,128]{3,2,1,0:T(8,128)(2,1)S(1)} %pad_maximum_fusion.q_ref, bf16[2,128,1024]{2,1,0:T(8,128)(2,1)S(1)} %attend_up.1.after_ref, ...), custom_call_target="tpu_custom_call" | custom-call | flops 1 | bytes 1 | tf_op jit(solution)/shard_map/attend_down/pallas_call | solution.py:216
  99.3 3.0 %project_up.1.after_ref = bf16[128,4096]{1,0:T(8,128)(2,1)S(1)} custom-call(s32[5]{0:T(128)S(1)} %pad_add_fusion.place, bf16[128,1024]{1,0:T(8,128)(2,1)S(1)} %get-tuple-element.30.mine_ref, bf16[128,1024]{1,0:T(8,128)(2,1)S(1)} %collective-permute-done.13.theirs_ref, bf16[2048,4096]{1,0:T(8,128)(2,1)S(1)} %hold_weight.1.after_ref.held_ref, ...), custom_call_target="tpu_custom_call" | custom-call | flops 1 | bytes 1 | tf_op jit(solution)/shard_map/project_up/pallas_call | solution.py:296
  102.3 3.0 %project_down.1.after_ref = bf16[128,4096]{1,0:T(8,128)(2,1)S(1)} custom-call(s32[5]{0:T(128)S(1)} %pad_add_fusion.place, bf16[128,1024]{1,0:T(8,128)(2,1)S(1)} %get-tuple-element.32.mine_ref, bf16[128,1024]{1,0:T(8,128)(2,1)S(1)} %collective-permute-done.12.theirs_ref, bf16[2048,4096]{1,0:T(8,128)(2,1)S(1)} %hold_weight.1.after_ref.held_ref, ...), custom_call_target="tpu_custom_call" | custom-call | flops 1 | bytes 1 | tf_op jit(solution)/shard_map/project_down/pallas_call | solution.py:296
  105.3 3.0 %collective-permute-start.18 = (bf16[128,4096]{1,0:T(8,128)(2,1)S(1)}, bf16[128,4096]{1,0:T(8,128)(2,1)S(1)}, u32[]{:S(2)}, u32[]{:S(2)}) collective-permute-start(bf16[128,4096]{1,0:T(8,128)(2,1)S(1)} %project_down.1.after_ref), channel_id=1, source_target_pairs={{0,3},{1,0},{2,1},{3,2},{4,7},{5,4},{6,5},{7,6},{8,11},{9,8},{10,9... | collective-permute-start | bytes 3145736 | tf_op jit(solution)/shard_map/ppermute | solution.py:336
  108.3 7.9 %attend_own.1.after_ref = bf16[2,128,1024]{2,1,0:T(8,128)(2,1)S(1)} custom-call(s32[1024]{0:T(1024)S(1)} %reshape.66.lists, s32[64]{0:T(128)S(1)} %reshape.67.counts, s32[5]{0:T(128)S(1)} %pad_add_fusion.place, bf16[2,8,512,128]{3,2,1,0:T(8,128)(2,1)S(1)} %pad_maximum_fusion.q_ref, bf16[128,4096]{1,0:T(8,128)(2,1)S(1)} %project_down.1.after_ref, ...), custom_call_target="tpu_custom_call" | custom-call | flops 1 | bytes 1 | tf_op jit(solution)/shard_map/attend_own/pallas_call | solution.py:216
  117.2 1.2 collective-permute-done.16.theirs_ref
  118.4 3.0 %project_own.1 = f32[128,4096]{1,0:T(8,128)S(1)} custom-call(s32[5]{0:T(128)S(1)} %pad_add_fusion.place, bf16[128,1024]{1,0:T(8,128)(2,1)S(1)} %get-tuple-element.28.mine_ref, bf16[128,1024]{1,0:T(8,128)(2,1)S(1)} %collective-permute-done.16.theirs_ref, bf16[2048,4096]{1,0:T(8,128)(2,1)S(1)} %hold_weight.1.after_ref.held_ref, ...), custom_call_target="tpu_custom_call" | custom-call | flops 1 | bytes 1 | tf_op jit(solution)/shard_map/project_own/pallas_call | solution.py:296
  121.4 9.1 %collective-permute-done.18 = bf16[128,4096]{1,0:T(8,128)(2,1)S(1)} collective-permute-done((bf16[128,4096]{1,0:T(8,128)(2,1)S(1)}, bf16[128,4096]{1,0:T(8,128)(2,1)S(1)}, u32[]{:S(2)}, u32[]{:S(2)}) %collective-permute-start.18) | collective-permute-done | bytes 1048608 | tf_op jit(solution)/shard_map/ppermute | solution.py:336
  130.5 3.1 %collective-permute-done.17 = bf16[128,4096]{1,0:T(8,128)(2,1)S(1)} collective-permute-done((bf16[128,4096]{1,0:T(8,128)(2,1)S(1)}, bf16[128,4096]{1,0:T(8,128)(2,1)S(1)}, u32[]{:S(2)}, u32[]{:S(2)}) %collective-permute-start.17) | collective-permute-done | bytes 1048608 | tf_op jit(solution)/shard_map/ppermute | solution.py:336
  133.6 1.4 %add_convert_fusion = bf16[128,4096]{1,0:T(8,128)(2,1)} fusion(bf16[128,4096]{1,0:T(8,128)(2,1)S(1)} %collective-permute-done.18, f32[128,4096]{1,0:T(8,128)S(1)} %project_own.1, bf16[128,4096]{1,0:T(8,128)(2,1)S(1)} %collective-permute-done.17), kind=kLoop, calls=%fused_computation.3 | loop fusion | flops 2621440 | bytes 5242880 | tf_op jit(solution)/shard_map/convert_element_type | solution.py:418
  (61 shorter events, 15.6 us)
Async XLA Ops:
  0.0 44.1 %copy-start = (s32[16,128,16]{1,2,0:T(8,128)S(1)}, s32[16,128,16]{1,2,0:T(8,128)}, u32[]{:S(2)}) copy-start(s32[16,128,16]{1,2,0:T(8,128)} %param.10) | copy-start | bytes 393220
  0.8 0.9 copy-start.2
  1.7 0.9 copy-start.3
  3.4 2.7 %collective-permute-start = (bf16[2,4,128,128]{3,2,1,0:T(8,128)(2,1)S(1)}, bf16[2,4,128,128]{3,2,1,0:T(8,128)(2,1)S(1)}, u32[]{:S(2)}, u32[]{:S(2)}) collective-permute-start(bf16[2,4,128,128]{3,2,1,0:T(8,128)(2,1)S(1)} %get-tuple-element.17), channel_id=1, source_target_pairs={{0,4},{4,0},{8,12},{12,8},{16,20},{20,16},{24,28},{28,24},{32,36},... | collective-permute-start | bytes 786440 | tf_op jit(solution)/shard_map/ppermute | solution.py:332
  6.1 10.7 %collective-permute-start.4 = (bf16[2,8,128,128]{3,2,1,0:T(8,128)(2,1)S(1)}, bf16[2,8,128,128]{3,2,1,0:T(8,128)(2,1)S(1)}, u32[]{:S(2)}, u32[]{:S(2)}) collective-permute-start(bf16[2,8,128,128]{3,2,1,0:T(8,128)(2,1)S(1)} %constant_dynamic-update-slice_fusion), channel_id=1, source_target_pairs={{0,16},{4,68},{8,24},{12,76},{16,0},{20,84},{24,8},{28,92},{32,48}... | collective-permute-start | bytes 1572872 | tf_op jit(solution)/shard_map/ppermute | solution.py:328
  9.8 13.1 %collective-permute-start.3 = (bf16[2,8,128,128]{3,2,1,0:T(8,128)(2,1)S(1)}, bf16[2,8,128,128]{3,2,1,0:T(8,128)(2,1)S(1)}, u32[]{:S(2)}, u32[]{:S(2)}) collective-permute-start(bf16[2,8,128,128]{3,2,1,0:T(8,128)(2,1)S(1)} %constant_dynamic-update-slice_fusion), channel_id=1, source_target_pairs={{0,24},{4,100},{8,0},{12,108},{16,8},{20,116},{24,16},{28,124},{32... | collective-permute-start | bytes 1572872 | tf_op jit(solution)/shard_map/ppermute | solution.py:328
  10.3 12.7 %collective-permute-start.1 = (bf16[2,8,128,128]{3,2,1,0:T(8,128)(2,1)S(1)}, bf16[2,8,128,128]{3,2,1,0:T(8,128)(2,1)S(1)}, u32[]{:S(2)}, u32[]{:S(2)}) collective-permute-start(bf16[2,8,128,128]{3,2,1,0:T(8,128)(2,1)S(1)} %constant_dynamic-update-slice_fusion), channel_id=1, source_target_pairs={{0,8},{4,36},{8,16},{12,44},{16,24},{20,52},{24,0},{28,60},{32,40}... | collective-permute-start | bytes 1572872 | tf_op jit(solution)/shard_map/ppermute | solution.py:328
  23.0 5.2 %copy-start.4 = (s32[16,128]{1,0:T(8,128)S(1)}, s32[16,128]{1,0:T(8,128)}, u32[]{:S(2)}) copy-start(s32[16,128]{1,0:T(8,128)} %param.11) | copy-start | bytes 24580
  24.1 15.5 %collective-permute-start.5 = (bf16[32,128,128]{2,1,0:T(8,128)(2,1)}, bf16[32,128,128]{2,1,0:T(8,128)(2,1)}, u32[]{:S(2)}, u32[]{:S(2)}) collective-permute-start(bf16[32,128,128]{2,1,0:T(8,128)(2,1)} %pad_maximum_fusion.1.refs_0_), channel_id=1, source_target_pairs={{0,32},{4,12},{8,40},{12,20},{16,48},{20,28},{24,56},{28,4},{32,64... | collective-permute-start | bytes 3145736 | tf_op jit(solution)/shard_map/ppermute | solution.py:328
  26.4 14.3 %collective-permute-start.7 = (bf16[32,128,128]{2,1,0:T(8,128)(2,1)}, bf16[32,128,128]{2,1,0:T(8,128)(2,1)}, u32[]{:S(2)}, u32[]{:S(2)}) collective-permute-start(bf16[32,128,128]{2,1,0:T(8,128)(2,1)} %pad_maximum_fusion.2.refs_3_), channel_id=1, source_target_pairs={{0,96},{4,28},{8,104},{12,4},{16,112},{20,12},{24,120},{28,20},{32... | collective-permute-start | bytes 3145736 | tf_op jit(solution)/shard_map/ppermute | solution.py:328
  28.3 23.6 %collective-permute-start.9 = (bf16[32,128,128]{2,1,0:T(8,128)(2,1)}, bf16[32,128,128]{2,1,0:T(8,128)(2,1)}, u32[]{:S(2)}, u32[]{:S(2)}) collective-permute-start(bf16[32,128,128]{2,1,0:T(8,128)(2,1)} %pad_maximum_fusion.1.refs_0_), channel_id=1, source_target_pairs={{0,96},{4,28},{8,104},{12,4},{16,112},{20,12},{24,120},{28,20},{32... | collective-permute-start | bytes 3145736 | tf_op jit(solution)/shard_map/ppermute | solution.py:328
  29.8 22.1 %collective-permute-start.10 = (bf16[32,128,128]{2,1,0:T(8,128)(2,1)}, bf16[32,128,128]{2,1,0:T(8,128)(2,1)}, u32[]{:S(2)}, u32[]{:S(2)}) collective-permute-start(bf16[32,128,128]{2,1,0:T(8,128)(2,1)} %pad_maximum_fusion.2.refs_3_), channel_id=1, source_target_pairs={{0,32},{4,12},{8,40},{12,20},{16,48},{20,28},{24,56},{28,4},{32,64... | collective-permute-start | bytes 3145736 | tf_op jit(solution)/shard_map/ppermute | solution.py:328
  32.0 22.8 %collective-permute-start.2 = (bf16[8,512,128]{2,1,0:T(8,128)(2,1)S(1)}, bf16[8,512,128]{2,1,0:T(8,128)(2,1)}, u32[]{:S(2)}, u32[]{:S(2)}) collective-permute-start(bf16[8,512,128]{2,1,0:T(8,128)(2,1)S(1)} %get-tuple-element.18), channel_id=1, source_target_pairs={{0,4},{4,0},{8,12},{12,8},{16,20},{20,16},{24,28},{28,24},{32,36},... | collective-permute-start | bytes 3145736 | tf_op jit(solution)/shard_map/ppermute | solution.py:332
  39.6 22.5 %collective-permute-start.6 = (bf16[32,128,128]{2,1,0:T(8,128)(2,1)}, bf16[32,128,128]{2,1,0:T(8,128)(2,1)}, u32[]{:S(2)}, u32[]{:S(2)}) collective-permute-start(bf16[32,128,128]{2,1,0:T(8,128)(2,1)} %collective-permute-done.5.refs_1_), channel_id=1, source_target_pairs={{0,32},{4,12},{8,40},{12,20},{16,48},{20,28},{24,56},{28,4},{32,64... | collective-permute-start | bytes 3145736 | tf_op jit(solution)/shard_map/ppermute | solution.py:328
  40.7 22.5 %collective-permute-start.8 = (bf16[32,128,128]{2,1,0:T(8,128)(2,1)}, bf16[32,128,128]{2,1,0:T(8,128)(2,1)}, u32[]{:S(2)}, u32[]{:S(2)}) collective-permute-start(bf16[32,128,128]{2,1,0:T(8,128)(2,1)} %collective-permute-done.7.refs_5_), channel_id=1, source_target_pairs={{0,96},{4,28},{8,104},{12,4},{16,112},{20,12},{24,120},{28,20},{32... | collective-permute-start | bytes 3145736 | tf_op jit(solution)/shard_map/ppermute | solution.py:328
  72.7 3.2 %collective-permute-start.11 = (bf16[128,1024]{1,0:T(8,128)(2,1)S(1)}, bf16[128,1024]{1,0:T(8,128)(2,1)S(1)}, u32[]{:S(2)}, u32[]{:S(2)}) collective-permute-start(bf16[128,1024]{1,0:T(8,128)(2,1)S(1)} %get-tuple-element.33), channel_id=1, source_target_pairs={{0,4},{4,0},{8,12},{12,8},{16,20},{20,16},{24,28},{28,24},{32,36},... | collective-permute-start | bytes 786440 | tf_op jit(solution)/shard_map/ppermute | solution.py:332
  79.0 23.3 %collective-permute-start.15 = (bf16[128,2048]{1,0:T(8,128)(2,1)S(1)}, bf16[128,2048]{1,0:T(8,128)(2,1)S(1)}, u32[]{:S(2)}, u32[]{:S(2)}) collective-permute-start(bf16[128,2048]{1,0:T(8,128)(2,1)S(1)} %get-tuple-element.26), channel_id=1, source_target_pairs={{0,3},{1,0},{2,1},{3,2},{4,7},{5,4},{6,5},{7,6},{8,11},{9,8},{10,9... | collective-permute-start | bytes 1572872 | tf_op jit(solution)/shard_map/ppermute | solution.py:336
  81.5 17.8 %collective-permute-start.14 = (bf16[128,2048]{1,0:T(8,128)(2,1)S(1)}, bf16[128,2048]{1,0:T(8,128)(2,1)S(1)}, u32[]{:S(2)}, u32[]{:S(2)}) collective-permute-start(bf16[128,2048]{1,0:T(8,128)(2,1)S(1)} %get-tuple-element.23.after_ref), channel_id=1, source_target_pairs={{0,1},{1,2},{2,3},{3,0},{4,5},{5,6},{6,7},{7,4},{8,9},{9,10},{10,1... | collective-permute-start | bytes 1572872 | tf_op jit(solution)/shard_map/ppermute | solution.py:336
  97.4 1.9 %collective-permute-start.13 = (bf16[128,1024]{1,0:T(8,128)(2,1)S(1)}, bf16[128,1024]{1,0:T(8,128)(2,1)S(1)}, u32[]{:S(2)}, u32[]{:S(2)}) collective-permute-start(bf16[128,1024]{1,0:T(8,128)(2,1)S(1)} %get-tuple-element.29), channel_id=1, source_target_pairs={{0,4},{4,0},{8,12},{12,8},{16,20},{20,16},{24,28},{28,24},{32,36},... | collective-permute-start | bytes 786440 | tf_op jit(solution)/shard_map/ppermute | solution.py:332
  98.1 4.1 %collective-permute-start.12 = (bf16[128,1024]{1,0:T(8,128)(2,1)S(1)}, bf16[128,1024]{1,0:T(8,128)(2,1)S(1)}, u32[]{:S(2)}, u32[]{:S(2)}) collective-permute-start(bf16[128,1024]{1,0:T(8,128)(2,1)S(1)} %get-tuple-element.31), channel_id=1, source_target_pairs={{0,4},{4,0},{8,12},{12,8},{16,20},{20,16},{24,28},{28,24},{32,36},... | collective-permute-start | bytes 786440 | tf_op jit(solution)/shard_map/ppermute | solution.py:332
  105.3 25.2 %collective-permute-start.18 = (bf16[128,4096]{1,0:T(8,128)(2,1)S(1)}, bf16[128,4096]{1,0:T(8,128)(2,1)S(1)}, u32[]{:S(2)}, u32[]{:S(2)}) collective-permute-start(bf16[128,4096]{1,0:T(8,128)(2,1)S(1)} %project_down.1.after_ref), channel_id=1, source_target_pairs={{0,3},{1,0},{2,1},{3,2},{4,7},{5,4},{6,5},{7,6},{8,11},{9,8},{10,9... | collective-permute-start | bytes 3145736 | tf_op jit(solution)/shard_map/ppermute | solution.py:336
  108.3 25.3 %collective-permute-start.17 = (bf16[128,4096]{1,0:T(8,128)(2,1)S(1)}, bf16[128,4096]{1,0:T(8,128)(2,1)S(1)}, u32[]{:S(2)}, u32[]{:S(2)}) collective-permute-start(bf16[128,4096]{1,0:T(8,128)(2,1)S(1)} %project_up.1.after_ref), channel_id=1, source_target_pairs={{0,1},{1,2},{2,3},{3,0},{4,5},{5,6},{6,7},{7,4},{8,9},{9,10},{10,1... | collective-permute-start | bytes 3145736 | tf_op jit(solution)/shard_map/ppermute | solution.py:336
  116.3 2.1 %collective-permute-start.16 = (bf16[128,1024]{1,0:T(8,128)(2,1)S(1)}, bf16[128,1024]{1,0:T(8,128)(2,1)S(1)}, u32[]{:S(2)}, u32[]{:S(2)}) collective-permute-start(bf16[128,1024]{1,0:T(8,128)(2,1)S(1)} %get-tuple-element.27), channel_id=1, source_target_pairs={{0,4},{4,0},{8,12},{12,8},{16,20},{20,16},{24,28},{28,24},{32,36},... | collective-permute-start | bytes 786440 | tf_op jit(solution)/shard_map/ppermute | solution.py:332
  118.4 16.6 %copy-start.1 = (s32[16,128,16]{1,2,0:T(8,128)S(1)}, s32[16,128,16]{1,2,0:T(8,128)}, u32[]{:S(2)}) copy-start(s32[16,128,16]{1,2,0:T(8,128)} %param.10) | copy-start | bytes 393220
